TPU v7x, 256 devices: a whole 4x4x8 slice. The times are simulated.
256 devices in a mesh: shard: 16 (over x, y), replica: 16 (over z, core).
Axes of the slice: x: 4, y: 4, z: 8, core: 2. Of those that a mesh axis runs over, the one named last changes fastest.
Arguments:
- grads: bfloat16 [16, 18432, 1024], P('replica', 'shard')
- assignment: int32 [18], replicated, may hold values from 0 to 31, as said below
- piece_slot: int32 [18], replicated, may hold values from 0 to 17, each once
- left_roots: bfloat16 [32, 1024, 1024], P('shard')
- right_roots: bfloat16 [32, 1024, 1024], P('shard')
Outputs:
- statistics: float32 [32, 2, 1024, 1024], P('shard', None, 'replica')
- direction: bfloat16 [18432, 1024], P('shard')
Inputs may be any that keep to these rules, and one draw needn't show every extreme that they name: `assignment`: values are distinct; in every draw some owner holds all 2 of its slots, and slot 31 is named. `piece_slot`: a permutation.
All inputs are finite; a program needn't handle non-finite values.
Results may differ from a plain program's by a relative error of at most 0.025.
Values may be sent and summed in bfloat16 or wider, within the bound.
No kernel may reach another device: no remote copies, remote signals or barrier semaphores. Data moves between devices by JAX's collectives and lax.ppermute only.
A program may use at most 128 MiB of HBM per device.

v0:
```python
import functools

import jax
import jax.numpy as jnp
from jax import lax
from jax.experimental import pallas as pl
from jax.experimental.pallas import tpu as pltpu
from jax.sharding import Mesh, PartitionSpec as P

epsilon = 1e-06
f32 = jnp.float32
bf16 = jnp.bfloat16

SHARDS, DEPTH, CORES = 16, 8, 2
SLOTS, BLOCKS, ROWS, WIDTH = 2, 18, 64, 1024
HALF = BLOCKS // CORES
CHUNK = WIDTH // DEPTH

ORDER = (4, 3, 5, 2, 6, 1, 7)
HOPS = (2, 6, 1, 7, 4, 3, 5, 0)

OWN, SEND, PLACE, KIND, OWNER, FILLED, SLOTKIND, PICK, USED, SIZE = 0, 9, 18, 34, 52, 70, 72, 74, 75, 128


def params(megabytes=32):
    return pltpu.CompilerParams(vmem_limit_bytes=megabytes * 1024 * 1024)


def cost(flops, moved):
    return pl.CostEstimate(flops=flops, bytes_accessed=moved, transcendentals=0)


def front_body(assignment, piece_slot, pieces, table, out, held, sem):
    shard, core = lax.axis_index("shard"), lax.axis_index("core")
    fetch = pltpu.make_async_copy(pieces, held, sem)
    fetch.start()

    for i in (*range(PLACE, PLACE + SHARDS), *range(FILLED, USED)):
        table[i] = 0
    slots = [assignment[k] for k in range(BLOCKS)]

    def block(k, unused):
        slot, place = assignment[k], piece_slot[k]
        rank = jnp.int32(0)
        for other in slots:
            rank += jnp.where(other < slot, 1, 0)
        kind, index = lax.rem(rank, CORES), lax.div(rank, CORES)
        owner, which = lax.div(slot, SLOTS), lax.rem(slot, SLOTS)
        table[jnp.where(kind == core, OWN, SEND) + index] = place
        table[KIND + place] = kind
        table[OWNER + place] = owner

        @pl.when(kind == core)
        def _():
            table[PLACE + owner] = index

        @pl.when(owner == shard)
        def _():
            table[FILLED + which] = 1
            table[SLOTKIND + which] = kind

        @pl.when((owner == shard) & (kind == core))
        def _():
            table[PICK] = which

        return unused

    lax.fori_loop(0, BLOCKS, block, 0)
    fetch.wait()
    for n in range(HALF):
        out[n] = held[table[SEND + n]]


def front(assignment, piece_slot, pieces):
    smem = pl.BlockSpec(memory_space=pltpu.SMEM)
    return pl.pallas_call(
        front_body,
        out_shape=(
            pltpu.HBM((SIZE,), jnp.int32),
            pltpu.VMEM((HALF, ROWS, WIDTH), bf16),
        ),
        in_specs=[smem, smem, pl.BlockSpec(memory_space=pl.ANY)],
        out_specs=(smem, pl.BlockSpec(memory_space=pltpu.VMEM)),
        scratch_shapes=[pltpu.VMEM((BLOCKS, ROWS, WIDTH), bf16), pltpu.SemaphoreType.DMA],
        compiler_params=params(56),
        cost_estimate=cost(0, 6 * BLOCKS * ROWS * WIDTH),
        name="front",
    )(assignment, piece_slot, pieces)


def pair_sum_body(table, pieces, other, *rest):
    sums, held = rest[:-1], rest[-1]
    me = lax.axis_index("z")

    def add(n, unused):
        held[...] = (pieces[table[OWN + n]].astype(f32) + other[n].astype(f32)).astype(bf16)
        for shift in range(DEPTH):
            target = lax.rem(me + shift, DEPTH)
            sums[shift][n] = held[:, pl.ds(pl.multiple_of(target * CHUNK, CHUNK), CHUNK)]
        return unused

    lax.fori_loop(0, HALF, add, 0)


def pair_sum(table, pieces, other):
    vmem = pl.BlockSpec(memory_space=pltpu.VMEM)
    return pl.pallas_call(
        pair_sum_body,
        out_shape=[jax.ShapeDtypeStruct((HALF, ROWS, CHUNK), bf16)] * DEPTH,
        in_specs=[pl.BlockSpec(memory_space=pltpu.SMEM), vmem, vmem],
        out_specs=[vmem] * DEPTH,
        scratch_shapes=[pltpu.VMEM((ROWS, WIDTH), bf16)],
        compiler_params=params(),
        cost_estimate=cost(HALF * ROWS * WIDTH, 6 * HALF * ROWS * WIDTH),
        name="pair_sum",
    )(table, pieces, other)


TEAM = 4


def route_own_body(table, pieces, routed):
    step = pl.program_id(0)
    for i in range(TEAM):
        routed[i, 0] = pieces[table[OWN + table[PLACE + TEAM * step + i]]]


def route_other_body(table, other, half, routed):
    step = pl.program_id(0)
    for i in range(TEAM):
        routed[i, 0] = other[table[PLACE + TEAM * step + i]]


def route(table, source, half=None):
    part = 0 if half is None else 1
    block = pl.BlockSpec((TEAM, 1, ROWS, WIDTH), lambda i, table: (i, part, 0, 0))
    return pl.pallas_call(
        route_other_body if part else route_own_body,
        out_shape=pltpu.HBM((SHARDS, CORES, ROWS, WIDTH), bf16),
        grid_spec=pltpu.PrefetchScalarGridSpec(
            num_scalar_prefetch=1,
            grid=(SHARDS // TEAM,),
            in_specs=[pl.BlockSpec(memory_space=pltpu.VMEM)] + [pl.BlockSpec(memory_space=pl.ANY)] * part,
            out_specs=block,
        ),
        input_output_aliases={2: 0} if part else {},
        compiler_params=params(),
        cost_estimate=cost(0, 4 * SHARDS * ROWS * WIDTH),
        name="route_other" if part else "route_own",
    )(table, source, *([half] if part else []))


def mean_body(*refs):
    parts, out = refs[:-1], refs[-1]
    for n in range(HALF):
        total = parts[0][n].astype(f32)
        for part in parts[1:]:
            total += part[n].astype(f32)
        out[n] = (total * (1.0 / (DEPTH * CORES))).astype(bf16)


def mean_of(parts):
    vmem = pl.BlockSpec(memory_space=pltpu.VMEM)
    return pl.pallas_call(
        mean_body,
        out_shape=jax.ShapeDtypeStruct((HALF, ROWS, CHUNK), bf16),
        in_specs=[vmem] * DEPTH,
        out_specs=vmem,
        compiler_params=params(),
        cost_estimate=cost(DEPTH * HALF * ROWS * CHUNK, 18 * HALF * ROWS * CHUNK),
        name="mean",
    )(*parts)


def mean_out_body(table, *refs):
    chunks, out = refs[:-1], refs[-1]
    me, step = lax.axis_index("z"), pl.program_id(0)

    def one(i, unused):
        index = table[PLACE + TEAM * step + i]
        for shift, chunk in zip(HOPS, chunks):
            source = lax.rem(me + DEPTH - shift, DEPTH)
            columns = pl.ds(pl.multiple_of(source * CHUNK, CHUNK), CHUNK)
            out[i, :, columns] = chunk[index]
        return unused

    lax.fori_loop(0, TEAM, one, 0)


def mean_out(table, chunks):
    return pl.pallas_call(
        mean_out_body,
        out_shape=pltpu.HBM((SHARDS, ROWS, WIDTH), bf16),
        grid_spec=pltpu.PrefetchScalarGridSpec(
            num_scalar_prefetch=1,
            grid=(SHARDS // TEAM,),
            in_specs=[pl.BlockSpec(memory_space=pltpu.VMEM)] * DEPTH,
            out_specs=pl.BlockSpec((TEAM, ROWS, WIDTH), lambda i, table: (i, 0, 0)),
        ),
        compiler_params=params(),
        cost_estimate=cost(0, 4 * SHARDS * ROWS * WIDTH),
        name="mean_out",
    )(table, *chunks)


STEPS = 4
STRIP = WIDTH // STEPS
LONG = WIDTH // 2


def precond_body(table, mean, left, right, out, roots, middle, scaled, sums, sems):
    slot = table[PICK]
    second = pltpu.make_async_copy(right.at[slot], roots.at[1], sems.at[STEPS])
    first = pltpu.make_async_copy(left.at[slot], roots.at[0], sems.at[STEPS + 1])
    second.start()
    first.start()
    sums[...] = jnp.zeros_like(sums)
    group = LONG // ROWS

    def power(step, unused):
        own = mean[pl.ds(pl.multiple_of(step * STRIP, STRIP), STRIP), :].astype(f32)
        sums[0:1, :] += jnp.sum(own * own, axis=0, keepdims=True)
        return unused

    lax.fori_loop(0, STEPS, power, 0)
    second.wait()

    def apply_right(step, unused):
        rows = pl.ds(pl.multiple_of(step * LONG, LONG), LONG)
        middle[rows, :] = jnp.dot(mean[rows, :], roots[1], preferred_element_type=f32).astype(bf16)
        return unused

    lax.fori_loop(0, WIDTH // LONG, apply_right, 0)
    first.wait()

    def apply_left(step, unused):
        rows = pl.ds(pl.multiple_of(step * LONG, LONG), LONG)
        product = jnp.dot(roots[0, rows, :], middle[...], preferred_element_type=f32).astype(bf16)
        wide = product.astype(f32)
        sums[1:2, :] += jnp.sum(wide * wide, axis=0, keepdims=True)
        scaled[pl.ds(step * group, group)] = product.reshape(group, ROWS, WIDTH)
        return unused

    lax.fori_loop(0, WIDTH // LONG, apply_left, 0)
    grad_power = jnp.sum(sums[0:1, :], axis=1, keepdims=True) * (1.0 / (WIDTH * WIDTH))
    pre_power = jnp.sum(sums[1:2, :], axis=1, keepdims=True) * (1.0 / (WIDTH * WIDTH))
    factor = jnp.sqrt((grad_power + epsilon) / (pre_power + epsilon))
    sends = []
    for step in range(STEPS):
        part = pl.ds(step * TEAM, TEAM)

        def scale(i, unused, step=step):
            scaled[step * TEAM + i] = (scaled[step * TEAM + i].astype(f32) * factor).astype(bf16)
            return unused

        lax.fori_loop(0, TEAM, scale, 0)
        sends.append(pltpu.make_async_copy(scaled.at[part], out.at[part], sems.at[step]))
        sends[-1].start()
    for send in sends:
        send.wait()


def precond(table, mean, left_roots, right_roots):
    anywhere = pl.BlockSpec(memory_space=pl.ANY)
    left_roots = pltpu.with_memory_space_constraint(left_roots, pltpu.HBM)
    right_roots = pltpu.with_memory_space_constraint(right_roots, pltpu.HBM)
    return pl.pallas_call(
        precond_body,
        out_shape=pltpu.HBM((SHARDS, ROWS, WIDTH), bf16),
        in_specs=[
            pl.BlockSpec(memory_space=pltpu.SMEM),
            pl.BlockSpec(memory_space=pltpu.VMEM),
            anywhere,
            anywhere,
        ],
        out_specs=anywhere,
        scratch_shapes=[
            pltpu.VMEM((2, WIDTH, WIDTH), bf16),
            pltpu.VMEM((WIDTH, WIDTH), bf16),
            pltpu.VMEM((SHARDS, ROWS, WIDTH), bf16),
            pltpu.VMEM((8, WIDTH), f32),
            pltpu.SemaphoreType.DMA((STEPS + 2,)),
        ],
        compiler_params=params(),
        cost_estimate=cost(80 * WIDTH**3, 8 * WIDTH**2),
        name="precond",
    )(table, mean, left_roots, right_roots)


def gram_body(grads, out, whole, terms, sems):
    scale = 1.0 / (WIDTH * DEPTH * CORES)
    per = STRIP // CHUNK
    for rep in range(CORES):
        whole[rep] = grads[:, rep].reshape(WIDTH, WIDTH)
    sends = []
    for step in range(STEPS):
        here = slice(step * STRIP, (step + 1) * STRIP)
        rest = slice(step * STRIP, WIDTH)
        left = right = None
        for rep in range(CORES):
            first = lax.dot_general(
                whole[rep, here, :], whole[rep, rest, :], (((1,), (1,)), ((), ())), preferred_element_type=f32
            )
            second = lax.dot_general(
                whole[rep, :, here], whole[rep, :, rest], (((0,), (0,)), ((), ())), preferred_element_type=f32
            )
            left = first if left is None else left + first
            right = second if right is None else right + second
        for side, value in enumerate((left, right)):
            value = value * scale
            terms[step * per : (step + 1) * per, side, :, rest] = value.astype(bf16).reshape(per, CHUNK, -1)
            for other in range(step + 1, STEPS):
                offset = (other - step) * STRIP
                cell = value[:, offset : offset + STRIP].T.astype(bf16).reshape(per, CHUNK, STRIP)
                terms[other * per : (other + 1) * per, side, :, here] = cell
        part = pl.ds(step * per, per)
        sends.append(pltpu.make_async_copy(terms.at[part], out.at[part], sems.at[step]))
        sends[-1].start()
    for send in sends:
        send.wait()


def gram(grads):
    return pl.pallas_call(
        gram_body,
        out_shape=pltpu.HBM((DEPTH, 2, CHUNK, WIDTH), bf16),
        in_specs=[pl.BlockSpec(memory_space=pltpu.VMEM)],
        out_specs=pl.BlockSpec(memory_space=pl.ANY),
        scratch_shapes=[
            pltpu.VMEM((CORES, WIDTH, WIDTH), bf16),
            pltpu.VMEM((DEPTH, 2, CHUNK, WIDTH), bf16),
            pltpu.SemaphoreType.DMA((STEPS,)),
        ],
        compiler_params=params(),
        cost_estimate=cost(8 * WIDTH**3, 8 * WIDTH**2),
        name="gram",
    )(grads)


GROUP = 6


def finish_body(table, returned, swapped, share, other, direction, statistics):
    core = lax.axis_index("core")
    step = pl.program_id(0)
    for i in range(GROUP):
        kind, owner = table[KIND + GROUP * step + i], table[OWNER + GROUP * step + i]

        @pl.when(kind == core)
        def _():
            direction[i] = returned[owner]

        @pl.when(kind != core)
        def _():
            direction[i] = swapped[owner]

    @pl.when(step == 0)
    def _():
        rows = pl.ds(pl.multiple_of(core * ROWS, ROWS), ROWS)
        for slot in range(SLOTS):
            for side in range(2):
                kept = share[side, rows, :].astype(f32)
                got = other[side, rows, :].astype(f32)
                value = jnp.where(table[SLOTKIND + slot] == core, kept, got)
                statistics[slot, side] = jnp.where(table[FILLED + slot] == 1, value, 0.0)


def finish(table, returned, swapped, share, other):
    return pl.pallas_call(
        finish_body,
        out_shape=(
            jax.ShapeDtypeStruct((BLOCKS, ROWS, WIDTH), bf16),
            jax.ShapeDtypeStruct((SLOTS, 2, ROWS, WIDTH), f32),
        ),
        grid_spec=pltpu.PrefetchScalarGridSpec(
            num_scalar_prefetch=1,
            grid=(BLOCKS // GROUP,),
            in_specs=[pl.BlockSpec(memory_space=pltpu.VMEM)] * 4,
            out_specs=(
                pl.BlockSpec((GROUP, ROWS, WIDTH), lambda i, table: (i, 0, 0)),
                pl.BlockSpec((SLOTS, 2, ROWS, WIDTH), lambda i, table: (0, 0, 0, 0)),
            ),
        ),
        compiler_params=params(),
        cost_estimate=cost(0, 24 * BLOCKS * ROWS * WIDTH),
        name="finish",
    )(table, returned, swapped, share, other)


def local(grads, assignment, piece_slot, left_roots, right_roots):
    swap = functools.partial(lax.ppermute, axis_name="core", perm=[(0, 1), (1, 0)])
    exchange = functools.partial(lax.all_to_all, axis_name="shard", split_axis=0, concat_axis=0, tiled=True)

    def along(array, shift):
        return lax.ppermute(array, "z", [(z, (z + shift) % DEPTH) for z in range(DEPTH)])

    pieces = grads.reshape(BLOCKS, ROWS, WIDTH)
    table, outgoing = front(assignment, piece_slot, pieces)
    table = pltpu.with_memory_space_constraint(table, pltpu.HBM)
    other = swap(outgoing)

    sums = pair_sum(table, pieces, other)
    parts = [sums[0]] + [along(sums[shift], shift) for shift in ORDER]
    owned = exchange(route(table, other, route(table, pieces)))
    chunk = mean_of(parts)
    chunks = {0: chunk} | {shift: along(chunk, shift) for shift in (2, 6, 1, 7)}
    chunks |= {4: along(chunks[2], 2), 3: along(chunks[2], 1), 5: along(chunks[6], 7)}
    chunks = [chunks[shift] for shift in HOPS]
    packed, owned = lax.optimization_barrier((mean_out(table, chunks), owned))
    mean = exchange(packed).reshape(WIDTH, WIDTH)

    terms = gram(owned)
    mean, unused = lax.optimization_barrier((mean, terms))
    share = lax.psum_scatter(terms.reshape(DEPTH * 2 * CHUNK, WIDTH), "z", scatter_dimension=0, tiled=True)
    share = share.reshape(2, CHUNK, WIDTH)

    returned = exchange(precond(table, mean, left_roots, right_roots))
    direction, statistics = finish(table, returned, swap(returned), share, swap(share))
    return statistics, direction.reshape(BLOCKS * ROWS, WIDTH)


def solution(mesh):
    fine = Mesh(mesh.devices.reshape(SHARDS, DEPTH, CORES), ("shard", "z", "core"))
    roots = P("shard", None, None)
    return jax.shard_map(
        local,
        mesh=fine,
        in_specs=(P(("z", "core"), "shard", None), P(), P(), roots, roots),
        out_specs=(P("shard", None, ("z", "core"), None), P("shard", None)),
        check_vma=False,
    )
```

profile of v0, /device:TPU:96, one launch (start us, length us, event | category | flops | bytes accessed | tf_op | source)
XLA Modules:
  0.0 177.8 jit_solution(2879823984895726436)
XLA Ops:
  7.2 3.0 %front.1 = (s32[128]{0:T(128)}, bf16[9,64,1024]{2,1,0:T(8,128)(2,1)S(1)}) custom-call(s32[18]{0:T(128)} %assignment.1, s32[18]{0:T(128)} %piece_slot.1, bf16[18,64,1024]{2,1,0:T(8,128)(2,1)} %bitcast.5), custom_call_target="tpu_custom_call" | custom-call | bytes 7077888 | tf_op jit(solution)/shard_map/front/pallas_call | solution.py:76
  10.3 2.6 %route_own.1.half = bf16[16,2,64,1024]{3,2,1,0:T(8,128)(2,1)} custom-call(s32[128]{0:T(128)} %get-tuple-element.17.table, bf16[18,64,1024]{2,1,0:T(8,128)(2,1)S(1)} %bitcast.6), custom_call_target="tpu_custom_call" | custom-call | bytes 4194304 | tf_op jit(solution)/shard_map/route_own/pallas_call | solution.py:137
  13.1 2.6 %route_other.1 = bf16[16,2,64,1024]{3,2,1,0:T(8,128)(2,1)} custom-call(s32[128]{0:T(128)} %get-tuple-element.17.table, bf16[9,64,1024]{2,1,0:T(8,128)(2,1)S(1)} %collective-permute-done.other, bf16[16,2,64,1024]{3,2,1,0:T(8,128)(2,1)} %route_own.1.half), custom_call_target="tpu_custom_call", output_to_operand_aliasing={{}: (2, {})} | custom-call | bytes 4194304 | tf_op jit(solution)/shard_map/route_other/pallas_call | solution.py:137
  15.7 7.1 %all-to-all-start = ((bf16[16,2,64,1024]{3,2,1,0:T(8,128)(2,1)}), bf16[16,2,64,1024]{3,2,1,0:T(8,128)(2,1)}, u32[]{:S(2)}, u32[]{:S(2)}) async-start(bf16[16,2,64,1024]{3,2,1,0:T(8,128)(2,1)} %route_other.1), calls=%async_computation | async-start | bytes 8388608 | tf_op jit(solution)/shard_map/all_to_all | solution.py:404
  22.8 1.4 pair_sum.1
  24.2 4.6 %collective-permute-start.1 = (bf16[9,64,128]{2,1,0:T(8,128)(2,1)S(1)}, bf16[9,64,128]{2,1,0:T(8,128)(2,1)S(1)}, u32[]{:S(2)}, u32[]{:S(2)}) collective-permute-start(bf16[9,64,128]{2,1,0:T(8,128)(2,1)S(1)} %get-tuple-element.20), channel_id=1, source_target_pairs={{0,8},{2,10},{4,12},{6,14},{8,0},{10,2},{12,4},{14,6},{1,9},{3,11}... | collective-permute-start | bytes 442376 | tf_op jit(solution)/shard_map/ppermute | solution.py:395
  28.9 3.7 %collective-permute-start.3 = (bf16[9,64,128]{2,1,0:T(8,128)(2,1)S(1)}, bf16[9,64,128]{2,1,0:T(8,128)(2,1)S(1)}, u32[]{:S(2)}, u32[]{:S(2)}) collective-permute-start(bf16[9,64,128]{2,1,0:T(8,128)(2,1)S(1)} %get-tuple-element.22), channel_id=1, source_target_pairs={{0,10},{2,12},{4,14},{6,0},{8,2},{10,4},{12,6},{14,8},{1,11},{3,13... | collective-permute-start | bytes 442376 | tf_op jit(solution)/shard_map/ppermute | solution.py:395
  32.6 0.8 collective-permute-start.4
  33.3 2.2 %collective-permute-start.5 = (bf16[9,64,128]{2,1,0:T(8,128)(2,1)S(1)}, bf16[9,64,128]{2,1,0:T(8,128)(2,1)S(1)}, u32[]{:S(2)}, u32[]{:S(2)}) collective-permute-start(bf16[9,64,128]{2,1,0:T(8,128)(2,1)S(1)} %get-tuple-element.24), channel_id=1, source_target_pairs={{0,12},{2,14},{4,0},{6,2},{8,4},{10,6},{12,8},{14,10},{1,13},{3,15... | collective-permute-start | bytes 442376 | tf_op jit(solution)/shard_map/ppermute | solution.py:395
  36.1 9.5 %collective-permute-start.6 = (bf16[9,64,128]{2,1,0:T(8,128)(2,1)S(1)}, bf16[9,64,128]{2,1,0:T(8,128)(2,1)S(1)}, u32[]{:S(2)}, u32[]{:S(2)}) collective-permute-start(bf16[9,64,128]{2,1,0:T(8,128)(2,1)S(1)} %get-tuple-element.25), channel_id=1, source_target_pairs={{0,2},{2,4},{4,6},{6,8},{8,10},{10,12},{12,14},{14,0},{1,3},{3,5},... | collective-permute-start | bytes 442376 | tf_op jit(solution)/shard_map/ppermute | solution.py:395
  45.6 1.4 collective-permute-done.2.refs_2_
  47.0 3.3 %collective-permute-start.7 = (bf16[9,64,128]{2,1,0:T(8,128)(2,1)S(1)}, bf16[9,64,128]{2,1,0:T(8,128)(2,1)S(1)}, u32[]{:S(2)}, u32[]{:S(2)}) collective-permute-start(bf16[9,64,128]{2,1,0:T(8,128)(2,1)S(1)} %get-tuple-element.26), channel_id=1, source_target_pairs={{0,14},{2,0},{4,2},{6,4},{8,6},{10,8},{12,10},{14,12},{1,15},{3,1}... | collective-permute-start | bytes 442376 | tf_op jit(solution)/shard_map/ppermute | solution.py:395
  50.4 1.8 %collective-permute-done.4.refs_4_ = bf16[9,64,128]{2,1,0:T(8,128)(2,1)S(1)} collective-permute-done((bf16[9,64,128]{2,1,0:T(8,128)(2,1)S(1)}, bf16[9,64,128]{2,1,0:T(8,128)(2,1)S(1)}, u32[]{:S(2)}, u32[]{:S(2)}) %collective-permute-start.4) | collective-permute-done | bytes 147488 | tf_op jit(solution)/shard_map/ppermute | solution.py:395
  52.2 3.4 %collective-permute-done.6.refs_6_ = bf16[9,64,128]{2,1,0:T(8,128)(2,1)S(1)} collective-permute-done((bf16[9,64,128]{2,1,0:T(8,128)(2,1)S(1)}, bf16[9,64,128]{2,1,0:T(8,128)(2,1)S(1)}, u32[]{:S(2)}, u32[]{:S(2)}) %collective-permute-start.6) | collective-permute-done | bytes 147488 | tf_op jit(solution)/shard_map/ppermute | solution.py:395
  55.8 0.8 collective-permute-start.9
  56.7 3.4 %collective-permute-start.8 = (bf16[9,64,128]{2,1,0:T(8,128)(2,1)S(1)}, bf16[9,64,128]{2,1,0:T(8,128)(2,1)S(1)}, u32[]{:S(2)}, u32[]{:S(2)}) collective-permute-start(bf16[9,64,128]{2,1,0:T(8,128)(2,1)S(1)} %mean.1.refs_7_), channel_id=1, source_target_pairs={{0,4},{2,6},{4,8},{6,10},{8,12},{10,14},{12,0},{14,2},{1,5},{3,7},... | collective-permute-start | bytes 442376 | tf_op jit(solution)/shard_map/ppermute | solution.py:395
  60.6 2.6 %collective-permute-start.10 = (bf16[9,64,128]{2,1,0:T(8,128)(2,1)S(1)}, bf16[9,64,128]{2,1,0:T(8,128)(2,1)S(1)}, u32[]{:S(2)}, u32[]{:S(2)}) collective-permute-start(bf16[9,64,128]{2,1,0:T(8,128)(2,1)S(1)} %mean.1.refs_7_), channel_id=1, source_target_pairs={{0,2},{2,4},{4,6},{6,8},{8,10},{10,12},{12,14},{14,0},{1,3},{3,5},... | collective-permute-start | bytes 442376 | tf_op jit(solution)/shard_map/ppermute | solution.py:395
  63.3 3.3 %collective-permute-done.9.refs_1_ = bf16[9,64,128]{2,1,0:T(8,128)(2,1)S(1)} collective-permute-done((bf16[9,64,128]{2,1,0:T(8,128)(2,1)S(1)}, bf16[9,64,128]{2,1,0:T(8,128)(2,1)S(1)}, u32[]{:S(2)}, u32[]{:S(2)}) %collective-permute-start.9) | collective-permute-done | bytes 147488 | tf_op jit(solution)/shard_map/ppermute | solution.py:395
  66.5 1.2 collective-permute-start.14
  67.8 3.3 %collective-permute-start.13 = (bf16[9,64,128]{2,1,0:T(8,128)(2,1)S(1)}, bf16[9,64,128]{2,1,0:T(8,128)(2,1)S(1)}, u32[]{:S(2)}, u32[]{:S(2)}) collective-permute-start(bf16[9,64,128]{2,1,0:T(8,128)(2,1)S(1)} %collective-permute-done.8.refs_0_), channel_id=1, source_target_pairs={{0,2},{2,4},{4,6},{6,8},{8,10},{10,12},{12,14},{14,0},{1,3},{3,5},... | collective-permute-start | bytes 442376 | tf_op jit(solution)/shard_map/ppermute | solution.py:395
  71.8 1.1 collective-permute-done.14.refs_6_
  72.9 2.3 %collective-permute-done.13.refs_5_ = bf16[9,64,128]{2,1,0:T(8,128)(2,1)S(1)} collective-permute-done((bf16[9,64,128]{2,1,0:T(8,128)(2,1)S(1)}, bf16[9,64,128]{2,1,0:T(8,128)(2,1)S(1)}, u32[]{:S(2)}, u32[]{:S(2)}) %collective-permute-start.13) | collective-permute-done | bytes 147488 | tf_op jit(solution)/shard_map/ppermute | solution.py:395
  75.2 4.7 %collective-permute-done.12.refs_4_ = bf16[9,64,128]{2,1,0:T(8,128)(2,1)S(1)} collective-permute-done((bf16[9,64,128]{2,1,0:T(8,128)(2,1)S(1)}, bf16[9,64,128]{2,1,0:T(8,128)(2,1)S(1)}, u32[]{:S(2)}, u32[]{:S(2)}) %collective-permute-start.12) | collective-permute-done | bytes 147488 | tf_op jit(solution)/shard_map/ppermute | solution.py:395
  79.9 2.9 %mean_out.1 = bf16[16,64,1024]{2,1,0:T(8,128)(2,1)} custom-call(s32[128]{0:T(128)} %get-tuple-element.17.table, bf16[9,64,128]{2,1,0:T(8,128)(2,1)S(1)} %collective-permute-done.8.refs_0_, bf16[9,64,128]{2,1,0:T(8,128)(2,1)S(1)} %collective-permute-done.9.refs_1_, bf16[9,64,128]{2,1,0:T(8,128)(2,1)S(1)} %collective-permute-done.10.refs_2_, ...), custom_call_target="tpu_custom_call" | custom-call | bytes 4194304 | tf_op jit(solution)/shard_map/mean_out/pallas_call | solution.py:191
  82.8 10.0 %all-to-all-start.1 = ((bf16[16,64,1024]{2,1,0:T(8,128)(2,1)}), bf16[16,64,1024]{2,1,0:T(8,128)(2,1)S(1)}, u32[]{:S(2)}, u32[]{:S(2)}) async-start(bf16[16,64,1024]{2,1,0:T(8,128)(2,1)} %mean_out.1), calls=%async_computation.1 | async-start | bytes 4194304 | tf_op jit(solution)/shard_map/all_to_all | solution.py:410
  92.8 9.0 %gram.1 = bf16[8,2,128,1024]{3,2,1,0:T(8,128)(2,1)} custom-call(bf16[16,2,64,1024]{3,2,1,0:T(8,128)(2,1)} %all-to-all-done.grads), custom_call_target="tpu_custom_call" | custom-call | flops 8589934592 | bytes 8388608 | tf_op jit(solution)/shard_map/gram/pallas_call | solution.py:324
  101.9 19.9 %all-to-all-done.1 = bf16[16,64,1024]{2,1,0:T(8,128)(2,1)S(1)} async-done(((bf16[16,64,1024]{2,1,0:T(8,128)(2,1)}), bf16[16,64,1024]{2,1,0:T(8,128)(2,1)S(1)}, u32[]{:S(2)}, u32[]{:S(2)}) %all-to-all-start.1) | async-done | bytes 2097184 | tf_op jit(solution)/shard_map/all_to_all | solution.py:410
  121.8 8.9 %precond.1 = bf16[16,64,1024]{2,1,0:T(8,128)(2,1)} custom-call(s32[128]{0:T(128)} %get-tuple-element.17.table, bf16[1024,1024]{1,0:T(8,128)(2,1)S(1)} %bitcast.8, bf16[2,1024,1024]{2,1,0:T(8,128)(2,1)} %left.1, bf16[2,1024,1024]{2,1,0:T(8,128)(2,1)} %right.1), custom_call_target="tpu_custom_call" | custom-call | flops 85899345920 | bytes 8388608 | tf_op jit(solution)/shard_map/precond/pallas_call | solution.py:267
  130.7 29.4 %all_to_all.15.returned = bf16[16,64,1024]{2,1,0:T(8,128)(2,1)S(1)} all-to-all(bf16[16,64,1024]{2,1,0:T(8,128)(2,1)} %precond.1), channel_id=1, replica_groups=mesh['shard'=16,'z'=8,'core'=2] {'shard'}, dimensions={0} | all-to-all | bytes 4194304 | tf_op jit(solution)/shard_map/all_to_all | solution.py:417
  160.6 4.5 %collective-permute-done.15.swapped = bf16[16,64,1024]{2,1,0:T(8,128)(2,1)} collective-permute-done((bf16[16,64,1024]{2,1,0:T(8,128)(2,1)S(1)}, bf16[16,64,1024]{2,1,0:T(8,128)(2,1)}, u32[]{:S(2)}, u32[]{:S(2)}) %collective-permute-start.15) | collective-permute-done | bytes 2097184 | tf_op jit(solution)/shard_map/ppermute | solution.py:418
  165.2 1.0 copy-done.1
  166.2 4.7 %finish.1 = (bf16[18,64,1024]{2,1,0:T(8,128)(2,1)}, f32[2,2,64,1024]{3,2,1,0:T(8,128)}) custom-call(s32[128]{0:T(128)} %get-tuple-element.17.table, bf16[16,64,1024]{2,1,0:T(8,128)(2,1)S(1)} %all_to_all.15.returned, bf16[16,64,1024]{2,1,0:T(8,128)(2,1)} %collective-permute-done.15.swapped, bf16[2,128,1024]{2,1,0:T(8,128)(2,1)S(1)} %bitcast.10, ...), custom_call_target="tpu_custom_call" | custom-call | bytes 28311552 | tf_op jit(solution)/shard_map/finish/pallas_call | solution.py:369
  (23 shorter events, 3.1 us)
Async XLA Ops:
  7.2 3.1 %copy-start = (bf16[1,1152,1024]{2,1,0:T(8,128)(2,1)S(1)}, bf16[1,1152,1024]{2,1,0:T(8,128)(2,1)}, u32[]{:S(2)}) copy-start(bf16[1,1152,1024]{2,1,0:T(8,128)(2,1)} %param.5) | copy-start | bytes 7077892
  10.2 2.9 %collective-permute-start = (bf16[9,64,1024]{2,1,0:T(8,128)(2,1)S(1)}, bf16[9,64,1024]{2,1,0:T(8,128)(2,1)S(1)}, u32[]{:S(2)}, u32[]{:S(2)}) collective-permute-start(bf16[9,64,1024]{2,1,0:T(8,128)(2,1)S(1)} %get-tuple-element.18), channel_id=1, source_target_pairs={{0,1},{1,0},{2,3},{3,2},{4,5},{5,4},{6,7},{7,6},{8,9},{9,8},{10,11... | collective-permute-start | bytes 3538952 | tf_op jit(solution)/shard_map/ppermute | solution.py:400
  15.7 67.1 %all-to-all-start = ((bf16[16,2,64,1024]{3,2,1,0:T(8,128)(2,1)}), bf16[16,2,64,1024]{3,2,1,0:T(8,128)(2,1)}, u32[]{:S(2)}, u32[]{:S(2)}) async-start(bf16[16,2,64,1024]{3,2,1,0:T(8,128)(2,1)} %route_other.1), calls=%async_computation | async-start | bytes 8388608 | tf_op jit(solution)/shard_map/all_to_all | solution.py:404
  24.2 12.0 %collective-permute-start.1 = (bf16[9,64,128]{2,1,0:T(8,128)(2,1)S(1)}, bf16[9,64,128]{2,1,0:T(8,128)(2,1)S(1)}, u32[]{:S(2)}, u32[]{:S(2)}) collective-permute-start(bf16[9,64,128]{2,1,0:T(8,128)(2,1)S(1)} %get-tuple-element.20), channel_id=1, source_target_pairs={{0,8},{2,10},{4,12},{6,14},{8,0},{10,2},{12,4},{14,6},{1,9},{3,11}... | collective-permute-start | bytes 442376 | tf_op jit(solution)/shard_map/ppermute | solution.py:395
  28.8 18.3 %collective-permute-start.2 = (bf16[9,64,128]{2,1,0:T(8,128)(2,1)S(1)}, bf16[9,64,128]{2,1,0:T(8,128)(2,1)S(1)}, u32[]{:S(2)}, u32[]{:S(2)}) collective-permute-start(bf16[9,64,128]{2,1,0:T(8,128)(2,1)S(1)} %get-tuple-element.21), channel_id=1, source_target_pairs={{0,6},{2,8},{4,10},{6,12},{8,14},{10,0},{12,2},{14,4},{1,7},{3,9},... | collective-permute-start | bytes 442376 | tf_op jit(solution)/shard_map/ppermute | solution.py:395
  28.9 21.5 %collective-permute-start.3 = (bf16[9,64,128]{2,1,0:T(8,128)(2,1)S(1)}, bf16[9,64,128]{2,1,0:T(8,128)(2,1)S(1)}, u32[]{:S(2)}, u32[]{:S(2)}) collective-permute-start(bf16[9,64,128]{2,1,0:T(8,128)(2,1)S(1)} %get-tuple-element.22), channel_id=1, source_target_pairs={{0,10},{2,12},{4,14},{6,0},{8,2},{10,4},{12,6},{14,8},{1,11},{3,13... | collective-permute-start | bytes 442376 | tf_op jit(solution)/shard_map/ppermute | solution.py:395
  32.6 19.6 %collective-permute-start.4 = (bf16[9,64,128]{2,1,0:T(8,128)(2,1)S(1)}, bf16[9,64,128]{2,1,0:T(8,128)(2,1)S(1)}, u32[]{:S(2)}, u32[]{:S(2)}) collective-permute-start(bf16[9,64,128]{2,1,0:T(8,128)(2,1)S(1)} %get-tuple-element.23), channel_id=1, source_target_pairs={{0,4},{2,6},{4,8},{6,10},{8,12},{10,14},{12,0},{14,2},{1,5},{3,7},... | collective-permute-start | bytes 442376 | tf_op jit(solution)/shard_map/ppermute | solution.py:395
  33.3 18.9 %collective-permute-start.5 = (bf16[9,64,128]{2,1,0:T(8,128)(2,1)S(1)}, bf16[9,64,128]{2,1,0:T(8,128)(2,1)S(1)}, u32[]{:S(2)}, u32[]{:S(2)}) collective-permute-start(bf16[9,64,128]{2,1,0:T(8,128)(2,1)S(1)} %get-tuple-element.24), channel_id=1, source_target_pairs={{0,12},{2,14},{4,0},{6,2},{8,4},{10,6},{12,8},{14,10},{1,13},{3,15... | collective-permute-start | bytes 442376 | tf_op jit(solution)/shard_map/ppermute | solution.py:395
  36.1 19.5 %collective-permute-start.6 = (bf16[9,64,128]{2,1,0:T(8,128)(2,1)S(1)}, bf16[9,64,128]{2,1,0:T(8,128)(2,1)S(1)}, u32[]{:S(2)}, u32[]{:S(2)}) collective-permute-start(bf16[9,64,128]{2,1,0:T(8,128)(2,1)S(1)} %get-tuple-element.25), channel_id=1, source_target_pairs={{0,2},{2,4},{4,6},{6,8},{8,10},{10,12},{12,14},{14,0},{1,3},{3,5},... | collective-permute-start | bytes 442376 | tf_op jit(solution)/shard_map/ppermute | solution.py:395
  47.0 8.6 %collective-permute-start.7 = (bf16[9,64,128]{2,1,0:T(8,128)(2,1)S(1)}, bf16[9,64,128]{2,1,0:T(8,128)(2,1)S(1)}, u32[]{:S(2)}, u32[]{:S(2)}) collective-permute-start(bf16[9,64,128]{2,1,0:T(8,128)(2,1)S(1)} %get-tuple-element.26), channel_id=1, source_target_pairs={{0,14},{2,0},{4,2},{6,4},{8,6},{10,8},{12,10},{14,12},{1,15},{3,1}... | collective-permute-start | bytes 442376 | tf_op jit(solution)/shard_map/ppermute | solution.py:395
  55.8 10.7 %collective-permute-start.9 = (bf16[9,64,128]{2,1,0:T(8,128)(2,1)S(1)}, bf16[9,64,128]{2,1,0:T(8,128)(2,1)S(1)}, u32[]{:S(2)}, u32[]{:S(2)}) collective-permute-start(bf16[9,64,128]{2,1,0:T(8,128)(2,1)S(1)} %mean.1.refs_7_), channel_id=1, source_target_pairs={{0,12},{2,14},{4,0},{6,2},{8,4},{10,6},{12,8},{14,10},{1,13},{3,15... | collective-permute-start | bytes 442376 | tf_op jit(solution)/shard_map/ppermute | solution.py:395
  56.7 11.1 %collective-permute-start.8 = (bf16[9,64,128]{2,1,0:T(8,128)(2,1)S(1)}, bf16[9,64,128]{2,1,0:T(8,128)(2,1)S(1)}, u32[]{:S(2)}, u32[]{:S(2)}) collective-permute-start(bf16[9,64,128]{2,1,0:T(8,128)(2,1)S(1)} %mean.1.refs_7_), channel_id=1, source_target_pairs={{0,4},{2,6},{4,8},{6,10},{8,12},{10,14},{12,0},{14,2},{1,5},{3,7},... | collective-permute-start | bytes 442376 | tf_op jit(solution)/shard_map/ppermute | solution.py:395
  60.0 11.8 %collective-permute-start.11 = (bf16[9,64,128]{2,1,0:T(8,128)(2,1)S(1)}, bf16[9,64,128]{2,1,0:T(8,128)(2,1)S(1)}, u32[]{:S(2)}, u32[]{:S(2)}) collective-permute-start(bf16[9,64,128]{2,1,0:T(8,128)(2,1)S(1)} %mean.1.refs_7_), channel_id=1, source_target_pairs={{0,14},{2,0},{4,2},{6,4},{8,6},{10,8},{12,10},{14,12},{1,15},{3,1}... | collective-permute-start | bytes 442376 | tf_op jit(solution)/shard_map/ppermute | solution.py:395
  60.6 11.2 %collective-permute-start.10 = (bf16[9,64,128]{2,1,0:T(8,128)(2,1)S(1)}, bf16[9,64,128]{2,1,0:T(8,128)(2,1)S(1)}, u32[]{:S(2)}, u32[]{:S(2)}) collective-permute-start(bf16[9,64,128]{2,1,0:T(8,128)(2,1)S(1)} %mean.1.refs_7_), channel_id=1, source_target_pairs={{0,2},{2,4},{4,6},{6,8},{8,10},{10,12},{12,14},{14,0},{1,3},{3,5},... | collective-permute-start | bytes 442376 | tf_op jit(solution)/shard_map/ppermute | solution.py:395
  66.5 6.4 %collective-permute-start.14 = (bf16[9,64,128]{2,1,0:T(8,128)(2,1)S(1)}, bf16[9,64,128]{2,1,0:T(8,128)(2,1)S(1)}, u32[]{:S(2)}, u32[]{:S(2)}) collective-permute-start(bf16[9,64,128]{2,1,0:T(8,128)(2,1)S(1)} %collective-permute-done.9.refs_1_), channel_id=1, source_target_pairs={{0,14},{2,0},{4,2},{6,4},{8,6},{10,8},{12,10},{14,12},{1,15},{3,1}... | collective-permute-start | bytes 442376 | tf_op jit(solution)/shard_map/ppermute | solution.py:395
  67.8 7.4 %collective-permute-start.13 = (bf16[9,64,128]{2,1,0:T(8,128)(2,1)S(1)}, bf16[9,64,128]{2,1,0:T(8,128)(2,1)S(1)}, u32[]{:S(2)}, u32[]{:S(2)}) collective-permute-start(bf16[9,64,128]{2,1,0:T(8,128)(2,1)S(1)} %collective-permute-done.8.refs_0_), channel_id=1, source_target_pairs={{0,2},{2,4},{4,6},{6,8},{8,10},{10,12},{12,14},{14,0},{1,3},{3,5},... | collective-permute-start | bytes 442376 | tf_op jit(solution)/shard_map/ppermute | solution.py:395
  71.1 8.8 %collective-permute-start.12 = (bf16[9,64,128]{2,1,0:T(8,128)(2,1)S(1)}, bf16[9,64,128]{2,1,0:T(8,128)(2,1)S(1)}, u32[]{:S(2)}, u32[]{:S(2)}) collective-permute-start(bf16[9,64,128]{2,1,0:T(8,128)(2,1)S(1)} %collective-permute-done.8.refs_0_), channel_id=1, source_target_pairs={{0,4},{2,6},{4,8},{6,10},{8,12},{10,14},{12,0},{14,2},{1,5},{3,7},... | collective-permute-start | bytes 442376 | tf_op jit(solution)/shard_map/ppermute | solution.py:395
  82.8 39.0 %all-to-all-start.1 = ((bf16[16,64,1024]{2,1,0:T(8,128)(2,1)}), bf16[16,64,1024]{2,1,0:T(8,128)(2,1)S(1)}, u32[]{:S(2)}, u32[]{:S(2)}) async-start(bf16[16,64,1024]{2,1,0:T(8,128)(2,1)} %mean_out.1), calls=%async_computation.1 | async-start | bytes 4194304 | tf_op jit(solution)/shard_map/all_to_all | solution.py:410
  92.8 67.3 %reduce-scatter.2.cloned.1.call-start = ((), (), s32[]{:S(2)}) async-start(), calls=%async_computation.4 | async-start | bytes 4718592 | tf_op jit(solution)/shard_map/reduce_scatter | solution.py:414
  160.1 5.0 %collective-permute-start.15 = (bf16[16,64,1024]{2,1,0:T(8,128)(2,1)S(1)}, bf16[16,64,1024]{2,1,0:T(8,128)(2,1)}, u32[]{:S(2)}, u32[]{:S(2)}) collective-permute-start(bf16[16,64,1024]{2,1,0:T(8,128)(2,1)S(1)} %all_to_all.15.returned), channel_id=1, source_target_pairs={{0,1},{1,0},{2,3},{3,2},{4,5},{5,4},{6,7},{7,6},{8,9},{9,8},{10,11... | collective-permute-start | bytes 6291464 | tf_op jit(solution)/shard_map/ppermute | solution.py:418
  160.1 5.0 %collective-permute-start.16 = (bf16[2,128,1024]{2,1,0:T(8,128)(2,1)}, bf16[2,128,1024]{2,1,0:T(8,128)(2,1)S(1)}, u32[]{:S(2)}, u32[]{:S(2)}) collective-permute-start(bf16[2,128,1024]{2,1,0:T(8,128)(2,1)} %bitcast.9), channel_id=1, source_target_pairs={{0,1},{1,0},{2,3},{3,2},{4,5},{5,4},{6,7},{7,6},{8,9},{9,8},{10,11... | collective-permute-start | bytes 1572872 | tf_op jit(solution)/shard_map/ppermute | solution.py:418
  165.2 1.0 copy-start.1
Sparse Core Ops, SparseCore 0:
  102.0 56.8 reduce-scatter.1
where the time goes:
time: 179 us; the launch traced here: 178 us
  starting transfers between devices  54.6 us (31%)
  waiting for transfers between devices  43.4 us (24%)
  Pallas kernels  35.2 us (20%)
  blocking collectives  29.4 us (16%)
  between operations  14.1 us (8%)
    ppermute x14, starting transfers between devices, along(): lax.ppermute(array, 'z', [(z, (z + shift) % DEPTH) for z in range(DEPTH)])  36.9 us
    all_to_all x1, blocking collectives, local(): returned = exchange(precond(table, mean, left_roots, right_roots))  29.4 us
    all_to_all x1, waiting for transfers between devices, local(): mean = exchange(packed).reshape(WIDTH, WIDTH)  19.9 us
    ppermute x14, waiting for transfers between devices, along(): lax.ppermute(array, 'z', [(z, (z + shift) % DEPTH) for z in range(DEPTH)])  18.7 us
    all_to_all x1, starting transfers between devices, local(): mean = exchange(packed).reshape(WIDTH, WIDTH)  10 us
    pallas_call x1, Pallas kernels, gram(): pl.pallas_call(gram_body, out_shape=pltpu.HBM((DEPTH, 2, CHUNK, WIDTH), b...  9 us
    pallas_call x1, Pallas kernels, precond(): pl.pallas_call(precond_body, out_shape=pltpu.HBM((SHARDS, ROWS, WIDTH), b...  8.91 us
    all_to_all x1, starting transfers between devices, local(): owned = exchange(route(table, other, route(table, pieces)))  7.09 us
  transfers between devices with their start and end apart: 20, of which 11 were waited for; matrix products, arithmetic and copies ran while one was open for 0% of the time, Pallas kernels for 14%

commit v1 on v0

--- a/solution.py
+++ b/solution.py
@@ -16,7 +16,7 @@
 HALF = BLOCKS // CORES
 CHUNK = WIDTH // DEPTH
 
-ORDER = (4, 3, 5, 2, 6, 1, 7)
+ORDER = (3, 5, 4, 2, 6, 1, 7)
 HOPS = (2, 6, 1, 7, 4, 3, 5, 0)
 
 OWN, SEND, PLACE, KIND, OWNER, FILLED, SLOTKIND, PICK, USED, SIZE = 0, 9, 18, 34, 52, 70, 72, 74, 75, 128

time: 179 us -> 180 us (level)
  starting transfers between devices: 54.6 us -> 42.2 us
  waiting for transfers between devices: 43.4 us -> 55.8 us
    ppermute x14, waiting for transfers between devices: 18.7 us -> 31.1 us  [along(): lax.ppermute(array, 'z', [(z, (z + shift) % DEPTH) for z in range(DEPTH)])]
    ppermute x14, starting transfers between devices: 36.9 us -> 25.3 us  [along(): lax.ppermute(array, 'z', [(z, (z + shift) % DEPTH) for z in range(DEPTH)])]
  transfers between devices with their start and end apart: 20 -> 20, of which waited for: 11 -> 12; matrix products, arithmetic and copies ran while one was open for 0% -> 0% of each run, Pallas kernels for 14% -> 14%
where the time goes in v1:
time: 180 us; the launch traced here: 178 us
  waiting for transfers between devices  55.8 us (31%)
  starting transfers between devices  42.2 us (23%)
  Pallas kernels  35.2 us (20%)
  blocking collectives  29.4 us (16%)
  between operations  14.1 us (8%)
    ppermute x14, waiting for transfers between devices, along(): lax.ppermute(array, 'z', [(z, (z + shift) % DEPTH) for z in range(DEPTH)])  31.1 us
    all_to_all x1, blocking collectives, local(): returned = exchange(precond(table, mean, left_roots, right_roots))  29.4 us
    ppermute x14, starting transfers between devices, along(): lax.ppermute(array, 'z', [(z, (z + shift) % DEPTH) for z in range(DEPTH)])  25.3 us
    all_to_all x1, waiting for transfers between devices, local(): mean = exchange(packed).reshape(WIDTH, WIDTH)  19.9 us
    all_to_all x1, starting transfers between devices, local(): mean = exchange(packed).reshape(WIDTH, WIDTH)  9.16 us
    pallas_call x1, Pallas kernels, gram(): pl.pallas_call(gram_body, out_shape=pltpu.HBM((DEPTH, 2, CHUNK, WIDTH), b...  9 us
    pallas_call x1, Pallas kernels, precond(): pl.pallas_call(precond_body, out_shape=pltpu.HBM((SHARDS, ROWS, WIDTH), b...  8.91 us
    all_to_all x1, starting transfers between devices, local(): owned = exchange(route(table, other, route(table, pieces)))  7.09 us
  transfers between devices with their start and end apart: 20, of which 12 were waited for; matrix products, arithmetic and copies ran while one was open for 0% of the time, Pallas kernels for 14%

profile of v1, /device:TPU:96, one launch (start us, length us, event | category | flops | bytes accessed | tf_op | source)
XLA Modules:
  0.0 177.8 jit_solution(9453786189248674439)
XLA Ops:
  7.2 3.0 %front.1 = (s32[128]{0:T(128)}, bf16[9,64,1024]{2,1,0:T(8,128)(2,1)S(1)}) custom-call(s32[18]{0:T(128)} %assignment.1, s32[18]{0:T(128)} %piece_slot.1, bf16[18,64,1024]{2,1,0:T(8,128)(2,1)} %bitcast.5), custom_call_target="tpu_custom_call" | custom-call | bytes 7077888 | tf_op jit(solution)/shard_map/front/pallas_call | solution.py:76
  10.3 2.6 %route_own.1.half = bf16[16,2,64,1024]{3,2,1,0:T(8,128)(2,1)} custom-call(s32[128]{0:T(128)} %get-tuple-element.17.table, bf16[18,64,1024]{2,1,0:T(8,128)(2,1)S(1)} %bitcast.6), custom_call_target="tpu_custom_call" | custom-call | bytes 4194304 | tf_op jit(solution)/shard_map/route_own/pallas_call | solution.py:137
  13.1 2.6 %route_other.1 = bf16[16,2,64,1024]{3,2,1,0:T(8,128)(2,1)} custom-call(s32[128]{0:T(128)} %get-tuple-element.17.table, bf16[9,64,1024]{2,1,0:T(8,128)(2,1)S(1)} %collective-permute-done.other, bf16[16,2,64,1024]{3,2,1,0:T(8,128)(2,1)} %route_own.1.half), custom_call_target="tpu_custom_call", output_to_operand_aliasing={{}: (2, {})} | custom-call | bytes 4194304 | tf_op jit(solution)/shard_map/route_other/pallas_call | solution.py:137
  15.7 7.1 %all-to-all-start = ((bf16[16,2,64,1024]{3,2,1,0:T(8,128)(2,1)}), bf16[16,2,64,1024]{3,2,1,0:T(8,128)(2,1)}, u32[]{:S(2)}, u32[]{:S(2)}) async-start(bf16[16,2,64,1024]{3,2,1,0:T(8,128)(2,1)} %route_other.1), calls=%async_computation | async-start | bytes 8388608 | tf_op jit(solution)/shard_map/all_to_all | solution.py:404
  22.8 1.4 pair_sum.1
  24.2 4.1 %collective-permute-start.1 = (bf16[9,64,128]{2,1,0:T(8,128)(2,1)S(1)}, bf16[9,64,128]{2,1,0:T(8,128)(2,1)S(1)}, u32[]{:S(2)}, u32[]{:S(2)}) collective-permute-start(bf16[9,64,128]{2,1,0:T(8,128)(2,1)S(1)} %get-tuple-element.20), channel_id=1, source_target_pairs={{0,6},{2,8},{4,10},{6,12},{8,14},{10,0},{12,2},{14,4},{1,7},{3,9},... | collective-permute-start | bytes 442376 | tf_op jit(solution)/shard_map/ppermute | solution.py:395
  28.3 4.3 %collective-permute-start.3 = (bf16[9,64,128]{2,1,0:T(8,128)(2,1)S(1)}, bf16[9,64,128]{2,1,0:T(8,128)(2,1)S(1)}, u32[]{:S(2)}, u32[]{:S(2)}) collective-permute-start(bf16[9,64,128]{2,1,0:T(8,128)(2,1)S(1)} %get-tuple-element.22), channel_id=1, source_target_pairs={{0,8},{2,10},{4,12},{6,14},{8,0},{10,2},{12,4},{14,6},{1,9},{3,11}... | collective-permute-start | bytes 442376 | tf_op jit(solution)/shard_map/ppermute | solution.py:395
  32.6 0.8 collective-permute-start.4
  33.4 2.1 %collective-permute-start.5 = (bf16[9,64,128]{2,1,0:T(8,128)(2,1)S(1)}, bf16[9,64,128]{2,1,0:T(8,128)(2,1)S(1)}, u32[]{:S(2)}, u32[]{:S(2)}) collective-permute-start(bf16[9,64,128]{2,1,0:T(8,128)(2,1)S(1)} %get-tuple-element.24), channel_id=1, source_target_pairs={{0,12},{2,14},{4,0},{6,2},{8,4},{10,6},{12,8},{14,10},{1,13},{3,15... | collective-permute-start | bytes 442376 | tf_op jit(solution)/shard_map/ppermute | solution.py:395
  35.5 3.5 %collective-permute-done.1.refs_1_ = bf16[9,64,128]{2,1,0:T(8,128)(2,1)S(1)} collective-permute-done((bf16[9,64,128]{2,1,0:T(8,128)(2,1)S(1)}, bf16[9,64,128]{2,1,0:T(8,128)(2,1)S(1)}, u32[]{:S(2)}, u32[]{:S(2)}) %collective-permute-start.1) | collective-permute-done | bytes 147488 | tf_op jit(solution)/shard_map/ppermute | solution.py:395
  39.0 3.3 %collective-permute-start.6 = (bf16[9,64,128]{2,1,0:T(8,128)(2,1)S(1)}, bf16[9,64,128]{2,1,0:T(8,128)(2,1)S(1)}, u32[]{:S(2)}, u32[]{:S(2)}) collective-permute-start(bf16[9,64,128]{2,1,0:T(8,128)(2,1)S(1)} %get-tuple-element.25), channel_id=1, source_target_pairs={{0,2},{2,4},{4,6},{6,8},{8,10},{10,12},{12,14},{14,0},{1,3},{3,5},... | collective-permute-start | bytes 442376 | tf_op jit(solution)/shard_map/ppermute | solution.py:395
  42.4 6.3 %collective-permute-done.2.refs_2_ = bf16[9,64,128]{2,1,0:T(8,128)(2,1)S(1)} collective-permute-done((bf16[9,64,128]{2,1,0:T(8,128)(2,1)S(1)}, bf16[9,64,128]{2,1,0:T(8,128)(2,1)S(1)}, u32[]{:S(2)}, u32[]{:S(2)}) %collective-permute-start.2) | collective-permute-done | bytes 147488 | tf_op jit(solution)/shard_map/ppermute | solution.py:395
  48.7 2.8 %collective-permute-done.4.refs_4_ = bf16[9,64,128]{2,1,0:T(8,128)(2,1)S(1)} collective-permute-done((bf16[9,64,128]{2,1,0:T(8,128)(2,1)S(1)}, bf16[9,64,128]{2,1,0:T(8,128)(2,1)S(1)}, u32[]{:S(2)}, u32[]{:S(2)}) %collective-permute-start.4) | collective-permute-done | bytes 147488 | tf_op jit(solution)/shard_map/ppermute | solution.py:395
  51.5 4.1 %collective-permute-done.5.refs_5_ = bf16[9,64,128]{2,1,0:T(8,128)(2,1)S(1)} collective-permute-done((bf16[9,64,128]{2,1,0:T(8,128)(2,1)S(1)}, bf16[9,64,128]{2,1,0:T(8,128)(2,1)S(1)}, u32[]{:S(2)}, u32[]{:S(2)}) %collective-permute-start.5) | collective-permute-done | bytes 147488 | tf_op jit(solution)/shard_map/ppermute | solution.py:395
  55.6 2.4 %collective-permute-done.7.refs_7_ = bf16[9,64,128]{2,1,0:T(8,128)(2,1)S(1)} collective-permute-done((bf16[9,64,128]{2,1,0:T(8,128)(2,1)S(1)}, bf16[9,64,128]{2,1,0:T(8,128)(2,1)S(1)}, u32[]{:S(2)}, u32[]{:S(2)}) %collective-permute-start.7) | collective-permute-done | bytes 147488 | tf_op jit(solution)/shard_map/ppermute | solution.py:395
  58.2 4.1 %collective-permute-start.8 = (bf16[9,64,128]{2,1,0:T(8,128)(2,1)S(1)}, bf16[9,64,128]{2,1,0:T(8,128)(2,1)S(1)}, u32[]{:S(2)}, u32[]{:S(2)}) collective-permute-start(bf16[9,64,128]{2,1,0:T(8,128)(2,1)S(1)} %mean.1.refs_7_), channel_id=1, source_target_pairs={{0,4},{2,6},{4,8},{6,10},{8,12},{10,14},{12,0},{14,2},{1,5},{3,7},... | collective-permute-start | bytes 442376 | tf_op jit(solution)/shard_map/ppermute | solution.py:395
  62.3 3.2 %collective-permute-start.10 = (bf16[9,64,128]{2,1,0:T(8,128)(2,1)S(1)}, bf16[9,64,128]{2,1,0:T(8,128)(2,1)S(1)}, u32[]{:S(2)}, u32[]{:S(2)}) collective-permute-start(bf16[9,64,128]{2,1,0:T(8,128)(2,1)S(1)} %mean.1.refs_7_), channel_id=1, source_target_pairs={{0,2},{2,4},{4,6},{6,8},{8,10},{10,12},{12,14},{14,0},{1,3},{3,5},... | collective-permute-start | bytes 442376 | tf_op jit(solution)/shard_map/ppermute | solution.py:395
  65.6 4.1 %collective-permute-done.9.refs_1_ = bf16[9,64,128]{2,1,0:T(8,128)(2,1)S(1)} collective-permute-done((bf16[9,64,128]{2,1,0:T(8,128)(2,1)S(1)}, bf16[9,64,128]{2,1,0:T(8,128)(2,1)S(1)}, u32[]{:S(2)}, u32[]{:S(2)}) %collective-permute-start.9) | collective-permute-done | bytes 147488 | tf_op jit(solution)/shard_map/ppermute | solution.py:395
  69.7 3.2 %collective-permute-start.13 = (bf16[9,64,128]{2,1,0:T(8,128)(2,1)S(1)}, bf16[9,64,128]{2,1,0:T(8,128)(2,1)S(1)}, u32[]{:S(2)}, u32[]{:S(2)}) collective-permute-start(bf16[9,64,128]{2,1,0:T(8,128)(2,1)S(1)} %collective-permute-done.8.refs_0_), channel_id=1, source_target_pairs={{0,2},{2,4},{4,6},{6,8},{8,10},{10,12},{12,14},{14,0},{1,3},{3,5},... | collective-permute-start | bytes 442376 | tf_op jit(solution)/shard_map/ppermute | solution.py:395
  73.0 3.1 %collective-permute-done.14.refs_6_ = bf16[9,64,128]{2,1,0:T(8,128)(2,1)S(1)} collective-permute-done((bf16[9,64,128]{2,1,0:T(8,128)(2,1)S(1)}, bf16[9,64,128]{2,1,0:T(8,128)(2,1)S(1)}, u32[]{:S(2)}, u32[]{:S(2)}) %collective-permute-start.14) | collective-permute-done | bytes 147488 | tf_op jit(solution)/shard_map/ppermute | solution.py:395
  76.1 2.1 %collective-permute-done.13.refs_5_ = bf16[9,64,128]{2,1,0:T(8,128)(2,1)S(1)} collective-permute-done((bf16[9,64,128]{2,1,0:T(8,128)(2,1)S(1)}, bf16[9,64,128]{2,1,0:T(8,128)(2,1)S(1)}, u32[]{:S(2)}, u32[]{:S(2)}) %collective-permute-start.13) | collective-permute-done | bytes 147488 | tf_op jit(solution)/shard_map/ppermute | solution.py:395
  78.2 2.6 %collective-permute-done.12.refs_4_ = bf16[9,64,128]{2,1,0:T(8,128)(2,1)S(1)} collective-permute-done((bf16[9,64,128]{2,1,0:T(8,128)(2,1)S(1)}, bf16[9,64,128]{2,1,0:T(8,128)(2,1)S(1)}, u32[]{:S(2)}, u32[]{:S(2)}) %collective-permute-start.12) | collective-permute-done | bytes 147488 | tf_op jit(solution)/shard_map/ppermute | solution.py:395
  80.8 2.9 %mean_out.1 = bf16[16,64,1024]{2,1,0:T(8,128)(2,1)} custom-call(s32[128]{0:T(128)} %get-tuple-element.17.table, bf16[9,64,128]{2,1,0:T(8,128)(2,1)S(1)} %collective-permute-done.8.refs_0_, bf16[9,64,128]{2,1,0:T(8,128)(2,1)S(1)} %collective-permute-done.9.refs_1_, bf16[9,64,128]{2,1,0:T(8,128)(2,1)S(1)} %collective-permute-done.10.refs_2_, ...), custom_call_target="tpu_custom_call" | custom-call | bytes 4194304 | tf_op jit(solution)/shard_map/mean_out/pallas_call | solution.py:191
  83.6 9.2 %all-to-all-start.1 = ((bf16[16,64,1024]{2,1,0:T(8,128)(2,1)}), bf16[16,64,1024]{2,1,0:T(8,128)(2,1)S(1)}, u32[]{:S(2)}, u32[]{:S(2)}) async-start(bf16[16,64,1024]{2,1,0:T(8,128)(2,1)} %mean_out.1), calls=%async_computation.1 | async-start | bytes 4194304 | tf_op jit(solution)/shard_map/all_to_all | solution.py:410
  92.8 9.0 %gram.1 = bf16[8,2,128,1024]{3,2,1,0:T(8,128)(2,1)} custom-call(bf16[16,2,64,1024]{3,2,1,0:T(8,128)(2,1)} %all-to-all-done.grads), custom_call_target="tpu_custom_call" | custom-call | flops 8589934592 | bytes 8388608 | tf_op jit(solution)/shard_map/gram/pallas_call | solution.py:324
  101.9 19.9 %all-to-all-done.1 = bf16[16,64,1024]{2,1,0:T(8,128)(2,1)S(1)} async-done(((bf16[16,64,1024]{2,1,0:T(8,128)(2,1)}), bf16[16,64,1024]{2,1,0:T(8,128)(2,1)S(1)}, u32[]{:S(2)}, u32[]{:S(2)}) %all-to-all-start.1) | async-done | bytes 2097184 | tf_op jit(solution)/shard_map/all_to_all | solution.py:410
  121.8 8.9 %precond.1 = bf16[16,64,1024]{2,1,0:T(8,128)(2,1)} custom-call(s32[128]{0:T(128)} %get-tuple-element.17.table, bf16[1024,1024]{1,0:T(8,128)(2,1)S(1)} %bitcast.8, bf16[2,1024,1024]{2,1,0:T(8,128)(2,1)} %left.1, bf16[2,1024,1024]{2,1,0:T(8,128)(2,1)} %right.1), custom_call_target="tpu_custom_call" | custom-call | flops 85899345920 | bytes 8388608 | tf_op jit(solution)/shard_map/precond/pallas_call | solution.py:267
  130.7 29.4 %all_to_all.15.returned = bf16[16,64,1024]{2,1,0:T(8,128)(2,1)S(1)} all-to-all(bf16[16,64,1024]{2,1,0:T(8,128)(2,1)} %precond.1), channel_id=1, replica_groups=mesh['shard'=16,'z'=8,'core'=2] {'shard'}, dimensions={0} | all-to-all | bytes 4194304 | tf_op jit(solution)/shard_map/all_to_all | solution.py:417
  160.1 0.5 collective-permute-start.16
  160.6 4.5 %collective-permute-done.15.swapped = bf16[16,64,1024]{2,1,0:T(8,128)(2,1)} collective-permute-done((bf16[16,64,1024]{2,1,0:T(8,128)(2,1)S(1)}, bf16[16,64,1024]{2,1,0:T(8,128)(2,1)}, u32[]{:S(2)}, u32[]{:S(2)}) %collective-permute-start.15) | collective-permute-done | bytes 2097184 | tf_op jit(solution)/shard_map/ppermute | solution.py:418
  165.2 1.0 copy-done.1
  166.2 4.7 %finish.1 = (bf16[18,64,1024]{2,1,0:T(8,128)(2,1)}, f32[2,2,64,1024]{3,2,1,0:T(8,128)}) custom-call(s32[128]{0:T(128)} %get-tuple-element.17.table, bf16[16,64,1024]{2,1,0:T(8,128)(2,1)S(1)} %all_to_all.15.returned, bf16[16,64,1024]{2,1,0:T(8,128)(2,1)} %collective-permute-done.15.swapped, bf16[2,128,1024]{2,1,0:T(8,128)(2,1)S(1)} %bitcast.10, ...), custom_call_target="tpu_custom_call" | custom-call | bytes 28311552 | tf_op jit(solution)/shard_map/finish/pallas_call | solution.py:369
  (23 shorter events, 0.7 us)
Async XLA Ops:
  7.2 3.1 %copy-start = (bf16[1,1152,1024]{2,1,0:T(8,128)(2,1)S(1)}, bf16[1,1152,1024]{2,1,0:T(8,128)(2,1)}, u32[]{:S(2)}) copy-start(bf16[1,1152,1024]{2,1,0:T(8,128)(2,1)} %param.5) | copy-start | bytes 7077892
  10.2 2.9 %collective-permute-start = (bf16[9,64,1024]{2,1,0:T(8,128)(2,1)S(1)}, bf16[9,64,1024]{2,1,0:T(8,128)(2,1)S(1)}, u32[]{:S(2)}, u32[]{:S(2)}) collective-permute-start(bf16[9,64,1024]{2,1,0:T(8,128)(2,1)S(1)} %get-tuple-element.18), channel_id=1, source_target_pairs={{0,1},{1,0},{2,3},{3,2},{4,5},{5,4},{6,7},{7,6},{8,9},{9,8},{10,11... | collective-permute-start | bytes 3538952 | tf_op jit(solution)/shard_map/ppermute | solution.py:400
  15.7 68.0 %all-to-all-start = ((bf16[16,2,64,1024]{3,2,1,0:T(8,128)(2,1)}), bf16[16,2,64,1024]{3,2,1,0:T(8,128)(2,1)}, u32[]{:S(2)}, u32[]{:S(2)}) async-start(bf16[16,2,64,1024]{3,2,1,0:T(8,128)(2,1)} %route_other.1), calls=%async_computation | async-start | bytes 8388608 | tf_op jit(solution)/shard_map/all_to_all | solution.py:404
  24.2 14.8 %collective-permute-start.1 = (bf16[9,64,128]{2,1,0:T(8,128)(2,1)S(1)}, bf16[9,64,128]{2,1,0:T(8,128)(2,1)S(1)}, u32[]{:S(2)}, u32[]{:S(2)}) collective-permute-start(bf16[9,64,128]{2,1,0:T(8,128)(2,1)S(1)} %get-tuple-element.20), channel_id=1, source_target_pairs={{0,6},{2,8},{4,10},{6,12},{8,14},{10,0},{12,2},{14,4},{1,7},{3,9},... | collective-permute-start | bytes 442376 | tf_op jit(solution)/shard_map/ppermute | solution.py:395
  28.3 20.4 %collective-permute-start.2 = (bf16[9,64,128]{2,1,0:T(8,128)(2,1)S(1)}, bf16[9,64,128]{2,1,0:T(8,128)(2,1)S(1)}, u32[]{:S(2)}, u32[]{:S(2)}) collective-permute-start(bf16[9,64,128]{2,1,0:T(8,128)(2,1)S(1)} %get-tuple-element.21), channel_id=1, source_target_pairs={{0,10},{2,12},{4,14},{6,0},{8,2},{10,4},{12,6},{14,8},{1,11},{3,13... | collective-permute-start | bytes 442376 | tf_op jit(solution)/shard_map/ppermute | solution.py:395
  28.3 20.4 %collective-permute-start.3 = (bf16[9,64,128]{2,1,0:T(8,128)(2,1)S(1)}, bf16[9,64,128]{2,1,0:T(8,128)(2,1)S(1)}, u32[]{:S(2)}, u32[]{:S(2)}) collective-permute-start(bf16[9,64,128]{2,1,0:T(8,128)(2,1)S(1)} %get-tuple-element.22), channel_id=1, source_target_pairs={{0,8},{2,10},{4,12},{6,14},{8,0},{10,2},{12,4},{14,6},{1,9},{3,11}... | collective-permute-start | bytes 442376 | tf_op jit(solution)/shard_map/ppermute | solution.py:395
  32.6 18.9 %collective-permute-start.4 = (bf16[9,64,128]{2,1,0:T(8,128)(2,1)S(1)}, bf16[9,64,128]{2,1,0:T(8,128)(2,1)S(1)}, u32[]{:S(2)}, u32[]{:S(2)}) collective-permute-start(bf16[9,64,128]{2,1,0:T(8,128)(2,1)S(1)} %get-tuple-element.23), channel_id=1, source_target_pairs={{0,4},{2,6},{4,8},{6,10},{8,12},{10,14},{12,0},{14,2},{1,5},{3,7},... | collective-permute-start | bytes 442376 | tf_op jit(solution)/shard_map/ppermute | solution.py:395
  33.4 22.2 %collective-permute-start.5 = (bf16[9,64,128]{2,1,0:T(8,128)(2,1)S(1)}, bf16[9,64,128]{2,1,0:T(8,128)(2,1)S(1)}, u32[]{:S(2)}, u32[]{:S(2)}) collective-permute-start(bf16[9,64,128]{2,1,0:T(8,128)(2,1)S(1)} %get-tuple-element.24), channel_id=1, source_target_pairs={{0,12},{2,14},{4,0},{6,2},{8,4},{10,6},{12,8},{14,10},{1,13},{3,15... | collective-permute-start | bytes 442376 | tf_op jit(solution)/shard_map/ppermute | solution.py:395
  39.0 16.6 %collective-permute-start.6 = (bf16[9,64,128]{2,1,0:T(8,128)(2,1)S(1)}, bf16[9,64,128]{2,1,0:T(8,128)(2,1)S(1)}, u32[]{:S(2)}, u32[]{:S(2)}) collective-permute-start(bf16[9,64,128]{2,1,0:T(8,128)(2,1)S(1)} %get-tuple-element.25), channel_id=1, source_target_pairs={{0,2},{2,4},{4,6},{6,8},{8,10},{10,12},{12,14},{14,0},{1,3},{3,5},... | collective-permute-start | bytes 442376 | tf_op jit(solution)/shard_map/ppermute | solution.py:395
  48.7 9.2 %collective-permute-start.7 = (bf16[9,64,128]{2,1,0:T(8,128)(2,1)S(1)}, bf16[9,64,128]{2,1,0:T(8,128)(2,1)S(1)}, u32[]{:S(2)}, u32[]{:S(2)}) collective-permute-start(bf16[9,64,128]{2,1,0:T(8,128)(2,1)S(1)} %get-tuple-element.26), channel_id=1, source_target_pairs={{0,14},{2,0},{4,2},{6,4},{8,6},{10,8},{12,10},{14,12},{1,15},{3,1}... | collective-permute-start | bytes 442376 | tf_op jit(solution)/shard_map/ppermute | solution.py:395
  58.1 11.6 %collective-permute-start.9 = (bf16[9,64,128]{2,1,0:T(8,128)(2,1)S(1)}, bf16[9,64,128]{2,1,0:T(8,128)(2,1)S(1)}, u32[]{:S(2)}, u32[]{:S(2)}) collective-permute-start(bf16[9,64,128]{2,1,0:T(8,128)(2,1)S(1)} %mean.1.refs_7_), channel_id=1, source_target_pairs={{0,12},{2,14},{4,0},{6,2},{8,4},{10,6},{12,8},{14,10},{1,13},{3,15... | collective-permute-start | bytes 442376 | tf_op jit(solution)/shard_map/ppermute | solution.py:395
  58.2 11.5 %collective-permute-start.8 = (bf16[9,64,128]{2,1,0:T(8,128)(2,1)S(1)}, bf16[9,64,128]{2,1,0:T(8,128)(2,1)S(1)}, u32[]{:S(2)}, u32[]{:S(2)}) collective-permute-start(bf16[9,64,128]{2,1,0:T(8,128)(2,1)S(1)} %mean.1.refs_7_), channel_id=1, source_target_pairs={{0,4},{2,6},{4,8},{6,10},{8,12},{10,14},{12,0},{14,2},{1,5},{3,7},... | collective-permute-start | bytes 442376 | tf_op jit(solution)/shard_map/ppermute | solution.py:395
  62.3 10.6 %collective-permute-start.11 = (bf16[9,64,128]{2,1,0:T(8,128)(2,1)S(1)}, bf16[9,64,128]{2,1,0:T(8,128)(2,1)S(1)}, u32[]{:S(2)}, u32[]{:S(2)}) collective-permute-start(bf16[9,64,128]{2,1,0:T(8,128)(2,1)S(1)} %mean.1.refs_7_), channel_id=1, source_target_pairs={{0,14},{2,0},{4,2},{6,4},{8,6},{10,8},{12,10},{14,12},{1,15},{3,1}... | collective-permute-start | bytes 442376 | tf_op jit(solution)/shard_map/ppermute | solution.py:395
  62.3 10.6 %collective-permute-start.10 = (bf16[9,64,128]{2,1,0:T(8,128)(2,1)S(1)}, bf16[9,64,128]{2,1,0:T(8,128)(2,1)S(1)}, u32[]{:S(2)}, u32[]{:S(2)}) collective-permute-start(bf16[9,64,128]{2,1,0:T(8,128)(2,1)S(1)} %mean.1.refs_7_), channel_id=1, source_target_pairs={{0,2},{2,4},{4,6},{6,8},{8,10},{10,12},{12,14},{14,0},{1,3},{3,5},... | collective-permute-start | bytes 442376 | tf_op jit(solution)/shard_map/ppermute | solution.py:395
  69.7 6.4 %collective-permute-start.14 = (bf16[9,64,128]{2,1,0:T(8,128)(2,1)S(1)}, bf16[9,64,128]{2,1,0:T(8,128)(2,1)S(1)}, u32[]{:S(2)}, u32[]{:S(2)}) collective-permute-start(bf16[9,64,128]{2,1,0:T(8,128)(2,1)S(1)} %collective-permute-done.9.refs_1_), channel_id=1, source_target_pairs={{0,14},{2,0},{4,2},{6,4},{8,6},{10,8},{12,10},{14,12},{1,15},{3,1}... | collective-permute-start | bytes 442376 | tf_op jit(solution)/shard_map/ppermute | solution.py:395
  69.7 8.5 %collective-permute-start.13 = (bf16[9,64,128]{2,1,0:T(8,128)(2,1)S(1)}, bf16[9,64,128]{2,1,0:T(8,128)(2,1)S(1)}, u32[]{:S(2)}, u32[]{:S(2)}) collective-permute-start(bf16[9,64,128]{2,1,0:T(8,128)(2,1)S(1)} %collective-permute-done.8.refs_0_), channel_id=1, source_target_pairs={{0,2},{2,4},{4,6},{6,8},{8,10},{10,12},{12,14},{14,0},{1,3},{3,5},... | collective-permute-start | bytes 442376 | tf_op jit(solution)/shard_map/ppermute | solution.py:395
  73.0 7.8 %collective-permute-start.12 = (bf16[9,64,128]{2,1,0:T(8,128)(2,1)S(1)}, bf16[9,64,128]{2,1,0:T(8,128)(2,1)S(1)}, u32[]{:S(2)}, u32[]{:S(2)}) collective-permute-start(bf16[9,64,128]{2,1,0:T(8,128)(2,1)S(1)} %collective-permute-done.8.refs_0_), channel_id=1, source_target_pairs={{0,4},{2,6},{4,8},{6,10},{8,12},{10,14},{12,0},{14,2},{1,5},{3,7},... | collective-permute-start | bytes 442376 | tf_op jit(solution)/shard_map/ppermute | solution.py:395
  83.6 38.2 %all-to-all-start.1 = ((bf16[16,64,1024]{2,1,0:T(8,128)(2,1)}), bf16[16,64,1024]{2,1,0:T(8,128)(2,1)S(1)}, u32[]{:S(2)}, u32[]{:S(2)}) async-start(bf16[16,64,1024]{2,1,0:T(8,128)(2,1)} %mean_out.1), calls=%async_computation.1 | async-start | bytes 4194304 | tf_op jit(solution)/shard_map/all_to_all | solution.py:410
  92.8 67.3 %reduce-scatter.2.cloned.1.call-start = ((), (), s32[]{:S(2)}) async-start(), calls=%async_computation.4 | async-start | bytes 4718592 | tf_op jit(solution)/shard_map/reduce_scatter | solution.py:414
  160.1 5.0 %collective-permute-start.15 = (bf16[16,64,1024]{2,1,0:T(8,128)(2,1)S(1)}, bf16[16,64,1024]{2,1,0:T(8,128)(2,1)}, u32[]{:S(2)}, u32[]{:S(2)}) collective-permute-start(bf16[16,64,1024]{2,1,0:T(8,128)(2,1)S(1)} %all_to_all.15.returned), channel_id=1, source_target_pairs={{0,1},{1,0},{2,3},{3,2},{4,5},{5,4},{6,7},{7,6},{8,9},{9,8},{10,11... | collective-permute-start | bytes 6291464 | tf_op jit(solution)/shard_map/ppermute | solution.py:418
  160.1 5.0 %collective-permute-start.16 = (bf16[2,128,1024]{2,1,0:T(8,128)(2,1)}, bf16[2,128,1024]{2,1,0:T(8,128)(2,1)S(1)}, u32[]{:S(2)}, u32[]{:S(2)}) collective-permute-start(bf16[2,128,1024]{2,1,0:T(8,128)(2,1)} %bitcast.9), channel_id=1, source_target_pairs={{0,1},{1,0},{2,3},{3,2},{4,5},{5,4},{6,7},{7,6},{8,9},{9,8},{10,11... | collective-permute-start | bytes 1572872 | tf_op jit(solution)/shard_map/ppermute | solution.py:418
  165.2 1.0 copy-start.1
Sparse Core Ops, SparseCore 0:
  102.0 56.8 reduce-scatter.1

commit v2 on v0

--- a/solution.py
+++ b/solution.py
@@ -17,9 +17,11 @@
 CHUNK = WIDTH // DEPTH
 
 ORDER = (4, 3, 5, 2, 6, 1, 7)
-HOPS = (2, 6, 1, 7, 4, 3, 5, 0)
-
-OWN, SEND, PLACE, KIND, OWNER, FILLED, SLOTKIND, PICK, USED, SIZE = 0, 9, 18, 34, 52, 70, 72, 74, 75, 128
+HOPS = (0, 2, 6, 1, 7, 4, 3, 5)
+DIRECT = 5
+
+OWN, SEND, PLACE, KIND, OWNER, FILLED, SLOTKIND, PICK, COLUMN = 0, 9, 18, 34, 52, 70, 72, 74, 75
+USED, SIZE = 75, 128
 
 
 def params(megabytes=32):
@@ -37,6 +39,8 @@
 
     for i in (*range(PLACE, PLACE + SHARDS), *range(FILLED, USED)):
         table[i] = 0
+    for i, shift in enumerate(HOPS):
+        table[COLUMN + i] = lax.rem(lax.axis_index("z") + DEPTH - shift, DEPTH)
     slots = [assignment[k] for k in range(BLOCKS)]
 
     def block(k, unused):
@@ -117,29 +121,30 @@
 
 
 TEAM = 4
+LOAD = 8
 
 
 def route_own_body(table, pieces, routed):
     step = pl.program_id(0)
-    for i in range(TEAM):
-        routed[i, 0] = pieces[table[OWN + table[PLACE + TEAM * step + i]]]
+    for i in range(LOAD):
+        routed[i, 0] = pieces[table[OWN + table[PLACE + LOAD * step + i]]]
 
 
 def route_other_body(table, other, half, routed):
     step = pl.program_id(0)
-    for i in range(TEAM):
-        routed[i, 0] = other[table[PLACE + TEAM * step + i]]
+    for i in range(LOAD):
+        routed[i, 0] = other[table[PLACE + LOAD * step + i]]
 
 
 def route(table, source, half=None):
     part = 0 if half is None else 1
-    block = pl.BlockSpec((TEAM, 1, ROWS, WIDTH), lambda i, table: (i, part, 0, 0))
+    block = pl.BlockSpec((LOAD, 1, ROWS, WIDTH), lambda i, table: (i, part, 0, 0))
     return pl.pallas_call(
         route_other_body if part else route_own_body,
         out_shape=pltpu.HBM((SHARDS, CORES, ROWS, WIDTH), bf16),
         grid_spec=pltpu.PrefetchScalarGridSpec(
             num_scalar_prefetch=1,
-            grid=(SHARDS // TEAM,),
+            grid=(SHARDS // LOAD,),
             in_specs=[pl.BlockSpec(memory_space=pltpu.VMEM)] + [pl.BlockSpec(memory_space=pl.ANY)] * part,
             out_specs=block,
         ),
@@ -172,35 +177,34 @@
     )(*parts)
 
 
-def mean_out_body(table, *refs):
-    chunks, out = refs[:-1], refs[-1]
-    me, step = lax.axis_index("z"), pl.program_id(0)
-
-    def one(i, unused):
-        index = table[PLACE + TEAM * step + i]
-        for shift, chunk in zip(HOPS, chunks):
-            source = lax.rem(me + DEPTH - shift, DEPTH)
-            columns = pl.ds(pl.multiple_of(source * CHUNK, CHUNK), CHUNK)
-            out[i, :, columns] = chunk[index]
-        return unused
-
-    lax.fori_loop(0, TEAM, one, 0)
-
-
-def mean_out(table, chunks):
-    return pl.pallas_call(
-        mean_out_body,
+def mean_out_body(table, *refs, count):
+    chunks, out = refs[:count], refs[-1]
+    for i, chunk in enumerate(chunks):
+
+        @pl.when(pl.program_id(0) == i)
+        def _(chunk=chunk):
+            for owner in range(SHARDS):
+                out[owner] = chunk[table[PLACE + owner]]
+
+
+def mean_out(table, chunks, half=None):
+    first, extra = (0, 0) if half is None else (DIRECT, 1)
+    count = len(chunks)
+    vmem, anywhere = pl.BlockSpec(memory_space=pltpu.VMEM), pl.BlockSpec(memory_space=pl.ANY)
+    return pl.pallas_call(
+        functools.partial(mean_out_body, count=count),
         out_shape=pltpu.HBM((SHARDS, ROWS, WIDTH), bf16),
         grid_spec=pltpu.PrefetchScalarGridSpec(
             num_scalar_prefetch=1,
-            grid=(SHARDS // TEAM,),
-            in_specs=[pl.BlockSpec(memory_space=pltpu.VMEM)] * DEPTH,
-            out_specs=pl.BlockSpec((TEAM, ROWS, WIDTH), lambda i, table: (i, 0, 0)),
+            grid=(count,),
+            in_specs=[vmem] * count + [anywhere] * extra,
+            out_specs=pl.BlockSpec((SHARDS, ROWS, CHUNK), lambda i, table: (0, 0, table[COLUMN + first + i])),
         ),
-        compiler_params=params(),
-        cost_estimate=cost(0, 4 * SHARDS * ROWS * WIDTH),
-        name="mean_out",
-    )(table, *chunks)
+        input_output_aliases={1 + count: 0} if extra else {},
+        compiler_params=params(),
+        cost_estimate=cost(0, 4 * SHARDS * ROWS * CHUNK * count),
+        name="mean_late" if extra else "mean_early",
+    )(table, *chunks, *([half] if extra else []))
 
 
 STEPS = 4
@@ -406,7 +410,8 @@
     chunks = {0: chunk} | {shift: along(chunk, shift) for shift in (2, 6, 1, 7)}
     chunks |= {4: along(chunks[2], 2), 3: along(chunks[2], 1), 5: along(chunks[6], 7)}
     chunks = [chunks[shift] for shift in HOPS]
-    packed, owned = lax.optimization_barrier((mean_out(table, chunks), owned))
+    packed = mean_out(table, chunks[DIRECT:], mean_out(table, chunks[:DIRECT]))
+    packed, owned = lax.optimization_barrier((packed, owned))
     mean = exchange(packed).reshape(WIDTH, WIDTH)
 
     terms = gram(owned)

time: 179 us -> 182 us (1.017)
  starting transfers between devices: 54.6 us -> 57.2 us
    ppermute x14, waiting for transfers between devices: 18.7 us -> 15.7 us  [along(): lax.ppermute(array, 'z', [(z, (z + shift) % DEPTH) for z in range(DEPTH)])]
    all_to_all x1, starting transfers between devices: 10 us -> 12.6 us  [local(): mean = exchange(packed).reshape(WIDTH, WIDTH)]
    pallas_call x1 -> x2, Pallas kernels: 2.86 us -> 5.04 us  [mean_out(): pl.pallas_call(functools.partial(mean_out_body, count=count), out_shape=p...]
  transfers between devices with their start and end apart: 20 -> 20, of which waited for: 11 -> 11; matrix products, arithmetic and copies ran while one was open for 0% -> 0% of each run, Pallas kernels for 14% -> 15%
where the time goes in v2:
time: 182 us; the launch traced here: 181 us
  starting transfers between devices  57.2 us (31%)
  waiting for transfers between devices  42.2 us (23%)
  Pallas kernels  36.5 us (20%)
  blocking collectives  29.6 us (16%)
  between operations  14.1 us (8%)
    ppermute x14, starting transfers between devices, along(): lax.ppermute(array, 'z', [(z, (z + shift) % DEPTH) for z in range(DEPTH)])  36.9 us
    all_to_all x1, blocking collectives, local(): returned = exchange(precond(table, mean, left_roots, right_roots))  29.6 us
    all_to_all x1, waiting for transfers between devices, local(): mean = exchange(packed).reshape(WIDTH, WIDTH)  19.8 us
    ppermute x14, waiting for transfers between devices, along(): lax.ppermute(array, 'z', [(z, (z + shift) % DEPTH) for z in range(DEPTH)])  15.7 us
    all_to_all x1, starting transfers between devices, local(): mean = exchange(packed).reshape(WIDTH, WIDTH)  12.6 us
    pallas_call x1, Pallas kernels, gram(): pl.pallas_call(gram_body, out_shape=pltpu.HBM((DEPTH, 2, CHUNK, WIDTH), b...  9 us
    pallas_call x1, Pallas kernels, precond(): pl.pallas_call(precond_body, out_shape=pltpu.HBM((SHARDS, ROWS, WIDTH), b...  8.91 us
    all_to_all x1, starting transfers between devices, local(): owned = exchange(route(table, other, route(table, pieces)))  7.09 us
  transfers between devices with their start and end apart: 20, of which 11 were waited for; matrix products, arithmetic and copies ran while one was open for 0% of the time, Pallas kernels for 15%

profile of v2, /device:TPU:96, one launch (start us, length us, event | category | flops | bytes accessed | tf_op | source)
XLA Modules:
  0.0 180.7 jit_solution(15341932408673547936)
XLA Ops:
  7.2 3.0 %front.1 = (s32[128]{0:T(128)}, bf16[9,64,1024]{2,1,0:T(8,128)(2,1)S(1)}) custom-call(s32[18]{0:T(128)} %assignment.1, s32[18]{0:T(128)} %piece_slot.1, bf16[18,64,1024]{2,1,0:T(8,128)(2,1)} %bitcast.5), custom_call_target="tpu_custom_call" | custom-call | bytes 7077888 | tf_op jit(solution)/shard_map/front/pallas_call | solution.py:80
  10.3 2.1 %route_own.1.half = bf16[16,2,64,1024]{3,2,1,0:T(8,128)(2,1)} custom-call(s32[128]{0:T(128)} %get-tuple-element.17.table, bf16[18,64,1024]{2,1,0:T(8,128)(2,1)S(1)} %bitcast.6), custom_call_target="tpu_custom_call" | custom-call | bytes 4194304 | tf_op jit(solution)/shard_map/route_own/pallas_call | solution.py:142
  13.1 2.1 %route_other.1 = bf16[16,2,64,1024]{3,2,1,0:T(8,128)(2,1)} custom-call(s32[128]{0:T(128)} %get-tuple-element.17.table, bf16[9,64,1024]{2,1,0:T(8,128)(2,1)S(1)} %collective-permute-done.other, bf16[16,2,64,1024]{3,2,1,0:T(8,128)(2,1)} %route_own.1.half), custom_call_target="tpu_custom_call", output_to_operand_aliasing={{}: (2, {})} | custom-call | bytes 4194304 | tf_op jit(solution)/shard_map/route_other/pallas_call | solution.py:142
  15.2 7.1 %all-to-all-start = ((bf16[16,2,64,1024]{3,2,1,0:T(8,128)(2,1)}), bf16[16,2,64,1024]{3,2,1,0:T(8,128)(2,1)}, u32[]{:S(2)}, u32[]{:S(2)}) async-start(bf16[16,2,64,1024]{3,2,1,0:T(8,128)(2,1)} %route_other.1), calls=%async_computation | async-start | bytes 8388608 | tf_op jit(solution)/shard_map/all_to_all | solution.py:408
  22.3 1.4 pair_sum.1
  23.8 4.6 %collective-permute-start.1 = (bf16[9,64,128]{2,1,0:T(8,128)(2,1)S(1)}, bf16[9,64,128]{2,1,0:T(8,128)(2,1)S(1)}, u32[]{:S(2)}, u32[]{:S(2)}) collective-permute-start(bf16[9,64,128]{2,1,0:T(8,128)(2,1)S(1)} %get-tuple-element.20), channel_id=1, source_target_pairs={{0,8},{2,10},{4,12},{6,14},{8,0},{10,2},{12,4},{14,6},{1,9},{3,11}... | collective-permute-start | bytes 442376 | tf_op jit(solution)/shard_map/ppermute | solution.py:399
  28.4 3.7 %collective-permute-start.3 = (bf16[9,64,128]{2,1,0:T(8,128)(2,1)S(1)}, bf16[9,64,128]{2,1,0:T(8,128)(2,1)S(1)}, u32[]{:S(2)}, u32[]{:S(2)}) collective-permute-start(bf16[9,64,128]{2,1,0:T(8,128)(2,1)S(1)} %get-tuple-element.22), channel_id=1, source_target_pairs={{0,10},{2,12},{4,14},{6,0},{8,2},{10,4},{12,6},{14,8},{1,11},{3,13... | collective-permute-start | bytes 442376 | tf_op jit(solution)/shard_map/ppermute | solution.py:399
  32.2 0.8 collective-permute-start.4
  32.9 2.2 %collective-permute-start.5 = (bf16[9,64,128]{2,1,0:T(8,128)(2,1)S(1)}, bf16[9,64,128]{2,1,0:T(8,128)(2,1)S(1)}, u32[]{:S(2)}, u32[]{:S(2)}) collective-permute-start(bf16[9,64,128]{2,1,0:T(8,128)(2,1)S(1)} %get-tuple-element.24), channel_id=1, source_target_pairs={{0,12},{2,14},{4,0},{6,2},{8,4},{10,6},{12,8},{14,10},{1,13},{3,15... | collective-permute-start | bytes 442376 | tf_op jit(solution)/shard_map/ppermute | solution.py:399
  35.6 9.6 %collective-permute-start.6 = (bf16[9,64,128]{2,1,0:T(8,128)(2,1)S(1)}, bf16[9,64,128]{2,1,0:T(8,128)(2,1)S(1)}, u32[]{:S(2)}, u32[]{:S(2)}) collective-permute-start(bf16[9,64,128]{2,1,0:T(8,128)(2,1)S(1)} %get-tuple-element.25), channel_id=1, source_target_pairs={{0,2},{2,4},{4,6},{6,8},{8,10},{10,12},{12,14},{14,0},{1,3},{3,5},... | collective-permute-start | bytes 442376 | tf_op jit(solution)/shard_map/ppermute | solution.py:399
  45.2 1.4 collective-permute-done.2.refs_2_
  46.6 3.2 %collective-permute-start.7 = (bf16[9,64,128]{2,1,0:T(8,128)(2,1)S(1)}, bf16[9,64,128]{2,1,0:T(8,128)(2,1)S(1)}, u32[]{:S(2)}, u32[]{:S(2)}) collective-permute-start(bf16[9,64,128]{2,1,0:T(8,128)(2,1)S(1)} %get-tuple-element.26), channel_id=1, source_target_pairs={{0,14},{2,0},{4,2},{6,4},{8,6},{10,8},{12,10},{14,12},{1,15},{3,1}... | collective-permute-start | bytes 442376 | tf_op jit(solution)/shard_map/ppermute | solution.py:399
  49.8 1.8 collective-permute-done.4.refs_4_
  51.6 3.5 %collective-permute-done.6.refs_6_ = bf16[9,64,128]{2,1,0:T(8,128)(2,1)S(1)} collective-permute-done((bf16[9,64,128]{2,1,0:T(8,128)(2,1)S(1)}, bf16[9,64,128]{2,1,0:T(8,128)(2,1)S(1)}, u32[]{:S(2)}, u32[]{:S(2)}) %collective-permute-start.6) | collective-permute-done | bytes 147488 | tf_op jit(solution)/shard_map/ppermute | solution.py:399
  55.3 0.8 collective-permute-start.11
  56.1 3.4 %collective-permute-start.8 = (bf16[9,64,128]{2,1,0:T(8,128)(2,1)S(1)}, bf16[9,64,128]{2,1,0:T(8,128)(2,1)S(1)}, u32[]{:S(2)}, u32[]{:S(2)}) collective-permute-start(bf16[9,64,128]{2,1,0:T(8,128)(2,1)S(1)} %mean.1.refs_0_), channel_id=1, source_target_pairs={{0,4},{2,6},{4,8},{6,10},{8,12},{10,14},{12,0},{14,2},{1,5},{3,7},... | collective-permute-start | bytes 442376 | tf_op jit(solution)/shard_map/ppermute | solution.py:399
  60.1 2.6 %collective-permute-start.13 = (bf16[9,64,128]{2,1,0:T(8,128)(2,1)S(1)}, bf16[9,64,128]{2,1,0:T(8,128)(2,1)S(1)}, u32[]{:S(2)}, u32[]{:S(2)}) collective-permute-start(bf16[9,64,128]{2,1,0:T(8,128)(2,1)S(1)} %mean.1.refs_0_), channel_id=1, source_target_pairs={{0,2},{2,4},{4,6},{6,8},{8,10},{10,12},{12,14},{14,0},{1,3},{3,5},... | collective-permute-start | bytes 442376 | tf_op jit(solution)/shard_map/ppermute | solution.py:399
  62.7 3.2 %collective-permute-done.11.refs_2_ = bf16[9,64,128]{2,1,0:T(8,128)(2,1)S(1)} collective-permute-done((bf16[9,64,128]{2,1,0:T(8,128)(2,1)S(1)}, bf16[9,64,128]{2,1,0:T(8,128)(2,1)S(1)}, u32[]{:S(2)}, u32[]{:S(2)}) %collective-permute-start.11) | collective-permute-done | bytes 147488 | tf_op jit(solution)/shard_map/ppermute | solution.py:399
  66.0 1.3 collective-permute-start.12
  67.2 3.3 %collective-permute-start.10 = (bf16[9,64,128]{2,1,0:T(8,128)(2,1)S(1)}, bf16[9,64,128]{2,1,0:T(8,128)(2,1)S(1)}, u32[]{:S(2)}, u32[]{:S(2)}) collective-permute-start(bf16[9,64,128]{2,1,0:T(8,128)(2,1)S(1)} %collective-permute-done.8.refs_1_), channel_id=1, source_target_pairs={{0,2},{2,4},{4,6},{6,8},{8,10},{10,12},{12,14},{14,0},{1,3},{3,5},... | collective-permute-start | bytes 442376 | tf_op jit(solution)/shard_map/ppermute | solution.py:399
  71.2 2.9 %mean_early.1.refs_3_ = bf16[16,64,1024]{2,1,0:T(8,128)(2,1)} custom-call(s32[128]{0:T(128)} %get-tuple-element.17.table, bf16[9,64,128]{2,1,0:T(8,128)(2,1)S(1)} %mean.1.refs_0_, bf16[9,64,128]{2,1,0:T(8,128)(2,1)S(1)} %collective-permute-done.8.refs_1_, bf16[9,64,128]{2,1,0:T(8,128)(2,1)S(1)} %collective-permute-done.11.refs_2_, ...), custom_call_target="tpu_custom_call" | custom-call | bytes 2621440 | tf_op jit(solution)/shard_map/mean_early/pallas_call | solution.py:194
  74.6 4.8 %collective-permute-done.9.refs_0_ = bf16[9,64,128]{2,1,0:T(8,128)(2,1)S(1)} collective-permute-done((bf16[9,64,128]{2,1,0:T(8,128)(2,1)S(1)}, bf16[9,64,128]{2,1,0:T(8,128)(2,1)S(1)}, u32[]{:S(2)}, u32[]{:S(2)}) %collective-permute-start.9) | collective-permute-done | bytes 147488 | tf_op jit(solution)/shard_map/ppermute | solution.py:399
  79.4 2.1 %mean_late.1 = bf16[16,64,1024]{2,1,0:T(8,128)(2,1)} custom-call(s32[128]{0:T(128)} %get-tuple-element.17.table, bf16[9,64,128]{2,1,0:T(8,128)(2,1)S(1)} %collective-permute-done.9.refs_0_, bf16[9,64,128]{2,1,0:T(8,128)(2,1)S(1)} %collective-permute-done.10.refs_1_, ...), custom_call_target="tpu_custom_call", output_to_operand_aliasing={{}: (4, {})} | custom-call | bytes 1572864 | tf_op jit(solution)/shard_map/mean_late/pallas_call | solution.py:194
  81.6 1.4 all-to-all-done.grads
  83.0 12.6 %all-to-all-start.1 = ((bf16[16,64,1024]{2,1,0:T(8,128)(2,1)}), bf16[16,64,1024]{2,1,0:T(8,128)(2,1)S(1)}, u32[]{:S(2)}, u32[]{:S(2)}) async-start(bf16[16,64,1024]{2,1,0:T(8,128)(2,1)} %mean_late.1), calls=%async_computation.1 | async-start | bytes 4194304 | tf_op jit(solution)/shard_map/all_to_all | solution.py:415
  95.7 9.0 %gram.1 = bf16[8,2,128,1024]{3,2,1,0:T(8,128)(2,1)} custom-call(bf16[16,2,64,1024]{3,2,1,0:T(8,128)(2,1)} %all-to-all-done.grads), custom_call_target="tpu_custom_call" | custom-call | flops 8589934592 | bytes 8388608 | tf_op jit(solution)/shard_map/gram/pallas_call | solution.py:328
  104.7 19.8 %all-to-all-done.1 = bf16[16,64,1024]{2,1,0:T(8,128)(2,1)S(1)} async-done(((bf16[16,64,1024]{2,1,0:T(8,128)(2,1)}), bf16[16,64,1024]{2,1,0:T(8,128)(2,1)S(1)}, u32[]{:S(2)}, u32[]{:S(2)}) %all-to-all-start.1) | async-done | bytes 2097184 | tf_op jit(solution)/shard_map/all_to_all | solution.py:415
  124.5 8.9 %precond.1 = bf16[16,64,1024]{2,1,0:T(8,128)(2,1)} custom-call(s32[128]{0:T(128)} %get-tuple-element.17.table, bf16[1024,1024]{1,0:T(8,128)(2,1)S(1)} %bitcast.8, bf16[2,1024,1024]{2,1,0:T(8,128)(2,1)} %left.1, bf16[2,1024,1024]{2,1,0:T(8,128)(2,1)} %right.1), custom_call_target="tpu_custom_call" | custom-call | flops 85899345920 | bytes 8388608 | tf_op jit(solution)/shard_map/precond/pallas_call | solution.py:271
  133.4 29.6 %all_to_all.15.returned = bf16[16,64,1024]{2,1,0:T(8,128)(2,1)S(1)} all-to-all(bf16[16,64,1024]{2,1,0:T(8,128)(2,1)} %precond.1), channel_id=1, replica_groups=mesh['shard'=16,'z'=8,'core'=2] {'shard'}, dimensions={0} | all-to-all | bytes 4194304 | tf_op jit(solution)/shard_map/all_to_all | solution.py:422
  163.5 4.5 %collective-permute-done.15.swapped = bf16[16,64,1024]{2,1,0:T(8,128)(2,1)} collective-permute-done((bf16[16,64,1024]{2,1,0:T(8,128)(2,1)S(1)}, bf16[16,64,1024]{2,1,0:T(8,128)(2,1)}, u32[]{:S(2)}, u32[]{:S(2)}) %collective-permute-start.15) | collective-permute-done | bytes 2097184 | tf_op jit(solution)/shard_map/ppermute | solution.py:423
  168.0 1.0 copy-done.1
  169.1 4.7 %finish.1 = (bf16[18,64,1024]{2,1,0:T(8,128)(2,1)}, f32[2,2,64,1024]{3,2,1,0:T(8,128)}) custom-call(s32[128]{0:T(128)} %get-tuple-element.17.table, bf16[16,64,1024]{2,1,0:T(8,128)(2,1)S(1)} %all_to_all.15.returned, bf16[16,64,1024]{2,1,0:T(8,128)(2,1)} %collective-permute-done.15.swapped, bf16[2,128,1024]{2,1,0:T(8,128)(2,1)S(1)} %bitcast.10, ...), custom_call_target="tpu_custom_call" | custom-call | bytes 28311552 | tf_op jit(solution)/shard_map/finish/pallas_call | solution.py:373
  (24 shorter events, 4.0 us)
Async XLA Ops:
  7.2 3.1 %copy-start = (bf16[1,1152,1024]{2,1,0:T(8,128)(2,1)S(1)}, bf16[1,1152,1024]{2,1,0:T(8,128)(2,1)}, u32[]{:S(2)}) copy-start(bf16[1,1152,1024]{2,1,0:T(8,128)(2,1)} %param.5) | copy-start | bytes 7077892
  10.2 2.9 %collective-permute-start = (bf16[9,64,1024]{2,1,0:T(8,128)(2,1)S(1)}, bf16[9,64,1024]{2,1,0:T(8,128)(2,1)S(1)}, u32[]{:S(2)}, u32[]{:S(2)}) collective-permute-start(bf16[9,64,1024]{2,1,0:T(8,128)(2,1)S(1)} %get-tuple-element.18), channel_id=1, source_target_pairs={{0,1},{1,0},{2,3},{3,2},{4,5},{5,4},{6,7},{7,6},{8,9},{9,8},{10,11... | collective-permute-start | bytes 3538952 | tf_op jit(solution)/shard_map/ppermute | solution.py:404
  15.2 67.7 %all-to-all-start = ((bf16[16,2,64,1024]{3,2,1,0:T(8,128)(2,1)}), bf16[16,2,64,1024]{3,2,1,0:T(8,128)(2,1)}, u32[]{:S(2)}, u32[]{:S(2)}) async-start(bf16[16,2,64,1024]{3,2,1,0:T(8,128)(2,1)} %route_other.1), calls=%async_computation | async-start | bytes 8388608 | tf_op jit(solution)/shard_map/all_to_all | solution.py:408
  23.8 11.8 %collective-permute-start.1 = (bf16[9,64,128]{2,1,0:T(8,128)(2,1)S(1)}, bf16[9,64,128]{2,1,0:T(8,128)(2,1)S(1)}, u32[]{:S(2)}, u32[]{:S(2)}) collective-permute-start(bf16[9,64,128]{2,1,0:T(8,128)(2,1)S(1)} %get-tuple-element.20), channel_id=1, source_target_pairs={{0,8},{2,10},{4,12},{6,14},{8,0},{10,2},{12,4},{14,6},{1,9},{3,11}... | collective-permute-start | bytes 442376 | tf_op jit(solution)/shard_map/ppermute | solution.py:399
  28.3 18.3 %collective-permute-start.2 = (bf16[9,64,128]{2,1,0:T(8,128)(2,1)S(1)}, bf16[9,64,128]{2,1,0:T(8,128)(2,1)S(1)}, u32[]{:S(2)}, u32[]{:S(2)}) collective-permute-start(bf16[9,64,128]{2,1,0:T(8,128)(2,1)S(1)} %get-tuple-element.21), channel_id=1, source_target_pairs={{0,6},{2,8},{4,10},{6,12},{8,14},{10,0},{12,2},{14,4},{1,7},{3,9},... | collective-permute-start | bytes 442376 | tf_op jit(solution)/shard_map/ppermute | solution.py:399
  28.4 21.4 %collective-permute-start.3 = (bf16[9,64,128]{2,1,0:T(8,128)(2,1)S(1)}, bf16[9,64,128]{2,1,0:T(8,128)(2,1)S(1)}, u32[]{:S(2)}, u32[]{:S(2)}) collective-permute-start(bf16[9,64,128]{2,1,0:T(8,128)(2,1)S(1)} %get-tuple-element.22), channel_id=1, source_target_pairs={{0,10},{2,12},{4,14},{6,0},{8,2},{10,4},{12,6},{14,8},{1,11},{3,13... | collective-permute-start | bytes 442376 | tf_op jit(solution)/shard_map/ppermute | solution.py:399
  32.2 19.4 %collective-permute-start.4 = (bf16[9,64,128]{2,1,0:T(8,128)(2,1)S(1)}, bf16[9,64,128]{2,1,0:T(8,128)(2,1)S(1)}, u32[]{:S(2)}, u32[]{:S(2)}) collective-permute-start(bf16[9,64,128]{2,1,0:T(8,128)(2,1)S(1)} %get-tuple-element.23), channel_id=1, source_target_pairs={{0,4},{2,6},{4,8},{6,10},{8,12},{10,14},{12,0},{14,2},{1,5},{3,7},... | collective-permute-start | bytes 442376 | tf_op jit(solution)/shard_map/ppermute | solution.py:399
  32.9 18.7 %collective-permute-start.5 = (bf16[9,64,128]{2,1,0:T(8,128)(2,1)S(1)}, bf16[9,64,128]{2,1,0:T(8,128)(2,1)S(1)}, u32[]{:S(2)}, u32[]{:S(2)}) collective-permute-start(bf16[9,64,128]{2,1,0:T(8,128)(2,1)S(1)} %get-tuple-element.24), channel_id=1, source_target_pairs={{0,12},{2,14},{4,0},{6,2},{8,4},{10,6},{12,8},{14,10},{1,13},{3,15... | collective-permute-start | bytes 442376 | tf_op jit(solution)/shard_map/ppermute | solution.py:399
  35.6 19.5 %collective-permute-start.6 = (bf16[9,64,128]{2,1,0:T(8,128)(2,1)S(1)}, bf16[9,64,128]{2,1,0:T(8,128)(2,1)S(1)}, u32[]{:S(2)}, u32[]{:S(2)}) collective-permute-start(bf16[9,64,128]{2,1,0:T(8,128)(2,1)S(1)} %get-tuple-element.25), channel_id=1, source_target_pairs={{0,2},{2,4},{4,6},{6,8},{8,10},{10,12},{12,14},{14,0},{1,3},{3,5},... | collective-permute-start | bytes 442376 | tf_op jit(solution)/shard_map/ppermute | solution.py:399
  46.6 8.5 %collective-permute-start.7 = (bf16[9,64,128]{2,1,0:T(8,128)(2,1)S(1)}, bf16[9,64,128]{2,1,0:T(8,128)(2,1)S(1)}, u32[]{:S(2)}, u32[]{:S(2)}) collective-permute-start(bf16[9,64,128]{2,1,0:T(8,128)(2,1)S(1)} %get-tuple-element.26), channel_id=1, source_target_pairs={{0,14},{2,0},{4,2},{6,4},{8,6},{10,8},{12,10},{14,12},{1,15},{3,1}... | collective-permute-start | bytes 442376 | tf_op jit(solution)/shard_map/ppermute | solution.py:399
  55.3 10.7 %collective-permute-start.11 = (bf16[9,64,128]{2,1,0:T(8,128)(2,1)S(1)}, bf16[9,64,128]{2,1,0:T(8,128)(2,1)S(1)}, u32[]{:S(2)}, u32[]{:S(2)}) collective-permute-start(bf16[9,64,128]{2,1,0:T(8,128)(2,1)S(1)} %mean.1.refs_0_), channel_id=1, source_target_pairs={{0,12},{2,14},{4,0},{6,2},{8,4},{10,6},{12,8},{14,10},{1,13},{3,15... | collective-permute-start | bytes 442376 | tf_op jit(solution)/shard_map/ppermute | solution.py:399
  56.1 11.1 %collective-permute-start.8 = (bf16[9,64,128]{2,1,0:T(8,128)(2,1)S(1)}, bf16[9,64,128]{2,1,0:T(8,128)(2,1)S(1)}, u32[]{:S(2)}, u32[]{:S(2)}) collective-permute-start(bf16[9,64,128]{2,1,0:T(8,128)(2,1)S(1)} %mean.1.refs_0_), channel_id=1, source_target_pairs={{0,4},{2,6},{4,8},{6,10},{8,12},{10,14},{12,0},{14,2},{1,5},{3,7},... | collective-permute-start | bytes 442376 | tf_op jit(solution)/shard_map/ppermute | solution.py:399
  59.5 11.8 %collective-permute-start.14 = (bf16[9,64,128]{2,1,0:T(8,128)(2,1)S(1)}, bf16[9,64,128]{2,1,0:T(8,128)(2,1)S(1)}, u32[]{:S(2)}, u32[]{:S(2)}) collective-permute-start(bf16[9,64,128]{2,1,0:T(8,128)(2,1)S(1)} %mean.1.refs_0_), channel_id=1, source_target_pairs={{0,14},{2,0},{4,2},{6,4},{8,6},{10,8},{12,10},{14,12},{1,15},{3,1}... | collective-permute-start | bytes 442376 | tf_op jit(solution)/shard_map/ppermute | solution.py:399
  60.1 11.2 %collective-permute-start.13 = (bf16[9,64,128]{2,1,0:T(8,128)(2,1)S(1)}, bf16[9,64,128]{2,1,0:T(8,128)(2,1)S(1)}, u32[]{:S(2)}, u32[]{:S(2)}) collective-permute-start(bf16[9,64,128]{2,1,0:T(8,128)(2,1)S(1)} %mean.1.refs_0_), channel_id=1, source_target_pairs={{0,2},{2,4},{4,6},{6,8},{8,10},{10,12},{12,14},{14,0},{1,3},{3,5},... | collective-permute-start | bytes 442376 | tf_op jit(solution)/shard_map/ppermute | solution.py:399
  66.0 8.2 %collective-permute-start.12 = (bf16[9,64,128]{2,1,0:T(8,128)(2,1)S(1)}, bf16[9,64,128]{2,1,0:T(8,128)(2,1)S(1)}, u32[]{:S(2)}, u32[]{:S(2)}) collective-permute-start(bf16[9,64,128]{2,1,0:T(8,128)(2,1)S(1)} %collective-permute-done.11.refs_2_), channel_id=1, source_target_pairs={{0,14},{2,0},{4,2},{6,4},{8,6},{10,8},{12,10},{14,12},{1,15},{3,1}... | collective-permute-start | bytes 442376 | tf_op jit(solution)/shard_map/ppermute | solution.py:399
  67.2 7.4 %collective-permute-start.10 = (bf16[9,64,128]{2,1,0:T(8,128)(2,1)S(1)}, bf16[9,64,128]{2,1,0:T(8,128)(2,1)S(1)}, u32[]{:S(2)}, u32[]{:S(2)}) collective-permute-start(bf16[9,64,128]{2,1,0:T(8,128)(2,1)S(1)} %collective-permute-done.8.refs_1_), channel_id=1, source_target_pairs={{0,2},{2,4},{4,6},{6,8},{8,10},{10,12},{12,14},{14,0},{1,3},{3,5},... | collective-permute-start | bytes 442376 | tf_op jit(solution)/shard_map/ppermute | solution.py:399
  70.5 8.9 %collective-permute-start.9 = (bf16[9,64,128]{2,1,0:T(8,128)(2,1)S(1)}, bf16[9,64,128]{2,1,0:T(8,128)(2,1)S(1)}, u32[]{:S(2)}, u32[]{:S(2)}) collective-permute-start(bf16[9,64,128]{2,1,0:T(8,128)(2,1)S(1)} %collective-permute-done.8.refs_1_), channel_id=1, source_target_pairs={{0,4},{2,6},{4,8},{6,10},{8,12},{10,14},{12,0},{14,2},{1,5},{3,7},... | collective-permute-start | bytes 442376 | tf_op jit(solution)/shard_map/ppermute | solution.py:399
  83.0 41.5 %all-to-all-start.1 = ((bf16[16,64,1024]{2,1,0:T(8,128)(2,1)}), bf16[16,64,1024]{2,1,0:T(8,128)(2,1)S(1)}, u32[]{:S(2)}, u32[]{:S(2)}) async-start(bf16[16,64,1024]{2,1,0:T(8,128)(2,1)} %mean_late.1), calls=%async_computation.1 | async-start | bytes 4194304 | tf_op jit(solution)/shard_map/all_to_all | solution.py:415
  95.6 67.4 %reduce-scatter.2.cloned.1.call-start = ((), (), s32[]{:S(2)}) async-start(), calls=%async_computation.4 | async-start | bytes 4718592 | tf_op jit(solution)/shard_map/reduce_scatter | solution.py:419
  163.0 5.0 %collective-permute-start.15 = (bf16[16,64,1024]{2,1,0:T(8,128)(2,1)S(1)}, bf16[16,64,1024]{2,1,0:T(8,128)(2,1)}, u32[]{:S(2)}, u32[]{:S(2)}) collective-permute-start(bf16[16,64,1024]{2,1,0:T(8,128)(2,1)S(1)} %all_to_all.15.returned), channel_id=1, source_target_pairs={{0,1},{1,0},{2,3},{3,2},{4,5},{5,4},{6,7},{7,6},{8,9},{9,8},{10,11... | collective-permute-start | bytes 6291464 | tf_op jit(solution)/shard_map/ppermute | solution.py:423
  163.0 5.0 %collective-permute-start.16 = (bf16[2,128,1024]{2,1,0:T(8,128)(2,1)}, bf16[2,128,1024]{2,1,0:T(8,128)(2,1)S(1)}, u32[]{:S(2)}, u32[]{:S(2)}) collective-permute-start(bf16[2,128,1024]{2,1,0:T(8,128)(2,1)} %bitcast.9), channel_id=1, source_target_pairs={{0,1},{1,0},{2,3},{3,2},{4,5},{5,4},{6,7},{7,6},{8,9},{9,8},{10,11... | collective-permute-start | bytes 1572872 | tf_op jit(solution)/shard_map/ppermute | solution.py:423
  168.0 1.0 copy-start.1
Sparse Core Ops, SparseCore 0:
  104.8 56.8 reduce-scatter.1

commit v3 on v0

--- a/solution.py
+++ b/solution.py
@@ -117,29 +117,30 @@
 
 
 TEAM = 4
+LOAD = 8
 
 
 def route_own_body(table, pieces, routed):
     step = pl.program_id(0)
-    for i in range(TEAM):
-        routed[i, 0] = pieces[table[OWN + table[PLACE + TEAM * step + i]]]
+    for i in range(LOAD):
+        routed[i, 0] = pieces[table[OWN + table[PLACE + LOAD * step + i]]]
 
 
 def route_other_body(table, other, half, routed):
     step = pl.program_id(0)
-    for i in range(TEAM):
-        routed[i, 0] = other[table[PLACE + TEAM * step + i]]
+    for i in range(LOAD):
+        routed[i, 0] = other[table[PLACE + LOAD * step + i]]
 
 
 def route(table, source, half=None):
     part = 0 if half is None else 1
-    block = pl.BlockSpec((TEAM, 1, ROWS, WIDTH), lambda i, table: (i, part, 0, 0))
+    block = pl.BlockSpec((LOAD, 1, ROWS, WIDTH), lambda i, table: (i, part, 0, 0))
     return pl.pallas_call(
         route_other_body if part else route_own_body,
         out_shape=pltpu.HBM((SHARDS, CORES, ROWS, WIDTH), bf16),
         grid_spec=pltpu.PrefetchScalarGridSpec(
             num_scalar_prefetch=1,
-            grid=(SHARDS // TEAM,),
+            grid=(SHARDS // LOAD,),
             in_specs=[pl.BlockSpec(memory_space=pltpu.VMEM)] + [pl.BlockSpec(memory_space=pl.ANY)] * part,
             out_specs=block,
         ),
@@ -337,7 +338,7 @@
     )(grads)
 
 
-GROUP = 6
+GROUP = 9
 
 
 def finish_body(table, returned, swapped, share, other, direction, statistics):

time: 179 us -> 182 us (1.017)
  starting transfers between devices: 54.6 us -> 57.4 us
    all_to_all x1, starting transfers between devices: 10 us -> 12.8 us  [local(): mean = exchange(packed).reshape(WIDTH, WIDTH)]
  transfers between devices with their start and end apart: 20 -> 20, of which waited for: 11 -> 12; matrix products, arithmetic and copies ran while one was open for 0% -> 0% of each run, Pallas kernels for 14% -> 14%
where the time goes in v3:
time: 182 us; the launch traced here: 180 us
  starting transfers between devices  57.4 us (32%)
  waiting for transfers between devices  44.4 us (24%)
  Pallas kernels  33.9 us (19%)
  blocking collectives  29.6 us (16%)
  between operations  14.1 us (8%)
    ppermute x14, starting transfers between devices, along(): lax.ppermute(array, 'z', [(z, (z + shift) % DEPTH) for z in range(DEPTH)])  36.9 us
    all_to_all x1, blocking collectives, local(): returned = exchange(precond(table, mean, left_roots, right_roots))  29.6 us
    all_to_all x1, waiting for transfers between devices, local(): mean = exchange(packed).reshape(WIDTH, WIDTH)  19.8 us
    ppermute x14, waiting for transfers between devices, along(): lax.ppermute(array, 'z', [(z, (z + shift) % DEPTH) for z in range(DEPTH)])  18.6 us
    all_to_all x1, starting transfers between devices, local(): mean = exchange(packed).reshape(WIDTH, WIDTH)  12.8 us
    pallas_call x1, Pallas kernels, gram(): pl.pallas_call(gram_body, out_shape=pltpu.HBM((DEPTH, 2, CHUNK, WIDTH), b...  9 us
    pallas_call x1, Pallas kernels, precond(): pl.pallas_call(precond_body, out_shape=pltpu.HBM((SHARDS, ROWS, WIDTH), b...  8.91 us
    all_to_all x1, starting transfers between devices, local(): owned = exchange(route(table, other, route(table, pieces)))  7.09 us
  transfers between devices with their start and end apart: 20, of which 12 were waited for; matrix products, arithmetic and copies ran while one was open for 0% of the time, Pallas kernels for 14%

profile of v3, /device:TPU:96, one launch (start us, length us, event | category | flops | bytes accessed | tf_op | source)
XLA Modules:
  0.0 180.4 jit_solution(11890817139331291352)
XLA Ops:
  7.2 3.0 %front.1 = (s32[128]{0:T(128)}, bf16[9,64,1024]{2,1,0:T(8,128)(2,1)S(1)}) custom-call(s32[18]{0:T(128)} %assignment.1, s32[18]{0:T(128)} %piece_slot.1, bf16[18,64,1024]{2,1,0:T(8,128)(2,1)} %bitcast.5), custom_call_target="tpu_custom_call" | custom-call | bytes 7077888 | tf_op jit(solution)/shard_map/front/pallas_call | solution.py:76
  10.3 2.1 %route_own.1.half = bf16[16,2,64,1024]{3,2,1,0:T(8,128)(2,1)} custom-call(s32[128]{0:T(128)} %get-tuple-element.17.table, bf16[18,64,1024]{2,1,0:T(8,128)(2,1)S(1)} %bitcast.6), custom_call_target="tpu_custom_call" | custom-call | bytes 4194304 | tf_op jit(solution)/shard_map/route_own/pallas_call | solution.py:138
  13.1 2.1 %route_other.1 = bf16[16,2,64,1024]{3,2,1,0:T(8,128)(2,1)} custom-call(s32[128]{0:T(128)} %get-tuple-element.17.table, bf16[9,64,1024]{2,1,0:T(8,128)(2,1)S(1)} %collective-permute-done.other, bf16[16,2,64,1024]{3,2,1,0:T(8,128)(2,1)} %route_own.1.half), custom_call_target="tpu_custom_call", output_to_operand_aliasing={{}: (2, {})} | custom-call | bytes 4194304 | tf_op jit(solution)/shard_map/route_other/pallas_call | solution.py:138
  15.2 7.1 %all-to-all-start = ((bf16[16,2,64,1024]{3,2,1,0:T(8,128)(2,1)}), bf16[16,2,64,1024]{3,2,1,0:T(8,128)(2,1)}, u32[]{:S(2)}, u32[]{:S(2)}) async-start(bf16[16,2,64,1024]{3,2,1,0:T(8,128)(2,1)} %route_other.1), calls=%async_computation | async-start | bytes 8388608 | tf_op jit(solution)/shard_map/all_to_all | solution.py:405
  22.3 1.4 pair_sum.1
  23.8 4.6 %collective-permute-start.1 = (bf16[9,64,128]{2,1,0:T(8,128)(2,1)S(1)}, bf16[9,64,128]{2,1,0:T(8,128)(2,1)S(1)}, u32[]{:S(2)}, u32[]{:S(2)}) collective-permute-start(bf16[9,64,128]{2,1,0:T(8,128)(2,1)S(1)} %get-tuple-element.20), channel_id=1, source_target_pairs={{0,8},{2,10},{4,12},{6,14},{8,0},{10,2},{12,4},{14,6},{1,9},{3,11}... | collective-permute-start | bytes 442376 | tf_op jit(solution)/shard_map/ppermute | solution.py:396
  28.4 3.7 %collective-permute-start.3 = (bf16[9,64,128]{2,1,0:T(8,128)(2,1)S(1)}, bf16[9,64,128]{2,1,0:T(8,128)(2,1)S(1)}, u32[]{:S(2)}, u32[]{:S(2)}) collective-permute-start(bf16[9,64,128]{2,1,0:T(8,128)(2,1)S(1)} %get-tuple-element.22), channel_id=1, source_target_pairs={{0,10},{2,12},{4,14},{6,0},{8,2},{10,4},{12,6},{14,8},{1,11},{3,13... | collective-permute-start | bytes 442376 | tf_op jit(solution)/shard_map/ppermute | solution.py:396
  32.2 0.8 collective-permute-start.4
  32.9 2.2 %collective-permute-start.5 = (bf16[9,64,128]{2,1,0:T(8,128)(2,1)S(1)}, bf16[9,64,128]{2,1,0:T(8,128)(2,1)S(1)}, u32[]{:S(2)}, u32[]{:S(2)}) collective-permute-start(bf16[9,64,128]{2,1,0:T(8,128)(2,1)S(1)} %get-tuple-element.24), channel_id=1, source_target_pairs={{0,12},{2,14},{4,0},{6,2},{8,4},{10,6},{12,8},{14,10},{1,13},{3,15... | collective-permute-start | bytes 442376 | tf_op jit(solution)/shard_map/ppermute | solution.py:396
  35.6 9.6 %collective-permute-start.6 = (bf16[9,64,128]{2,1,0:T(8,128)(2,1)S(1)}, bf16[9,64,128]{2,1,0:T(8,128)(2,1)S(1)}, u32[]{:S(2)}, u32[]{:S(2)}) collective-permute-start(bf16[9,64,128]{2,1,0:T(8,128)(2,1)S(1)} %get-tuple-element.25), channel_id=1, source_target_pairs={{0,2},{2,4},{4,6},{6,8},{8,10},{10,12},{12,14},{14,0},{1,3},{3,5},... | collective-permute-start | bytes 442376 | tf_op jit(solution)/shard_map/ppermute | solution.py:396
  45.2 1.4 collective-permute-done.2.refs_2_
  46.6 3.2 %collective-permute-start.7 = (bf16[9,64,128]{2,1,0:T(8,128)(2,1)S(1)}, bf16[9,64,128]{2,1,0:T(8,128)(2,1)S(1)}, u32[]{:S(2)}, u32[]{:S(2)}) collective-permute-start(bf16[9,64,128]{2,1,0:T(8,128)(2,1)S(1)} %get-tuple-element.26), channel_id=1, source_target_pairs={{0,14},{2,0},{4,2},{6,4},{8,6},{10,8},{12,10},{14,12},{1,15},{3,1}... | collective-permute-start | bytes 442376 | tf_op jit(solution)/shard_map/ppermute | solution.py:396
  49.8 1.8 collective-permute-done.4.refs_4_
  51.6 3.5 %collective-permute-done.6.refs_6_ = bf16[9,64,128]{2,1,0:T(8,128)(2,1)S(1)} collective-permute-done((bf16[9,64,128]{2,1,0:T(8,128)(2,1)S(1)}, bf16[9,64,128]{2,1,0:T(8,128)(2,1)S(1)}, u32[]{:S(2)}, u32[]{:S(2)}) %collective-permute-start.6) | collective-permute-done | bytes 147488 | tf_op jit(solution)/shard_map/ppermute | solution.py:396
  55.3 0.8 collective-permute-start.9
  56.1 3.4 %collective-permute-start.8 = (bf16[9,64,128]{2,1,0:T(8,128)(2,1)S(1)}, bf16[9,64,128]{2,1,0:T(8,128)(2,1)S(1)}, u32[]{:S(2)}, u32[]{:S(2)}) collective-permute-start(bf16[9,64,128]{2,1,0:T(8,128)(2,1)S(1)} %mean.1.refs_7_), channel_id=1, source_target_pairs={{0,4},{2,6},{4,8},{6,10},{8,12},{10,14},{12,0},{14,2},{1,5},{3,7},... | collective-permute-start | bytes 442376 | tf_op jit(solution)/shard_map/ppermute | solution.py:396
  60.1 2.6 %collective-permute-start.10 = (bf16[9,64,128]{2,1,0:T(8,128)(2,1)S(1)}, bf16[9,64,128]{2,1,0:T(8,128)(2,1)S(1)}, u32[]{:S(2)}, u32[]{:S(2)}) collective-permute-start(bf16[9,64,128]{2,1,0:T(8,128)(2,1)S(1)} %mean.1.refs_7_), channel_id=1, source_target_pairs={{0,2},{2,4},{4,6},{6,8},{8,10},{10,12},{12,14},{14,0},{1,3},{3,5},... | collective-permute-start | bytes 442376 | tf_op jit(solution)/shard_map/ppermute | solution.py:396
  62.7 3.2 %collective-permute-done.9.refs_1_ = bf16[9,64,128]{2,1,0:T(8,128)(2,1)S(1)} collective-permute-done((bf16[9,64,128]{2,1,0:T(8,128)(2,1)S(1)}, bf16[9,64,128]{2,1,0:T(8,128)(2,1)S(1)}, u32[]{:S(2)}, u32[]{:S(2)}) %collective-permute-start.9) | collective-permute-done | bytes 147488 | tf_op jit(solution)/shard_map/ppermute | solution.py:396
  66.0 1.3 collective-permute-start.14
  67.2 3.3 %collective-permute-start.13 = (bf16[9,64,128]{2,1,0:T(8,128)(2,1)S(1)}, bf16[9,64,128]{2,1,0:T(8,128)(2,1)S(1)}, u32[]{:S(2)}, u32[]{:S(2)}) collective-permute-start(bf16[9,64,128]{2,1,0:T(8,128)(2,1)S(1)} %collective-permute-done.8.refs_0_), channel_id=1, source_target_pairs={{0,2},{2,4},{4,6},{6,8},{8,10},{10,12},{12,14},{14,0},{1,3},{3,5},... | collective-permute-start | bytes 442376 | tf_op jit(solution)/shard_map/ppermute | solution.py:396
  71.2 1.1 collective-permute-done.14.refs_6_
  72.3 2.3 %collective-permute-done.13.refs_5_ = bf16[9,64,128]{2,1,0:T(8,128)(2,1)S(1)} collective-permute-done((bf16[9,64,128]{2,1,0:T(8,128)(2,1)S(1)}, bf16[9,64,128]{2,1,0:T(8,128)(2,1)S(1)}, u32[]{:S(2)}, u32[]{:S(2)}) %collective-permute-start.13) | collective-permute-done | bytes 147488 | tf_op jit(solution)/shard_map/ppermute | solution.py:396
  74.6 4.8 %collective-permute-done.12.refs_4_ = bf16[9,64,128]{2,1,0:T(8,128)(2,1)S(1)} collective-permute-done((bf16[9,64,128]{2,1,0:T(8,128)(2,1)S(1)}, bf16[9,64,128]{2,1,0:T(8,128)(2,1)S(1)}, u32[]{:S(2)}, u32[]{:S(2)}) %collective-permute-start.12) | collective-permute-done | bytes 147488 | tf_op jit(solution)/shard_map/ppermute | solution.py:396
  79.4 2.9 %mean_out.1 = bf16[16,64,1024]{2,1,0:T(8,128)(2,1)} custom-call(s32[128]{0:T(128)} %get-tuple-element.17.table, bf16[9,64,128]{2,1,0:T(8,128)(2,1)S(1)} %collective-permute-done.8.refs_0_, bf16[9,64,128]{2,1,0:T(8,128)(2,1)S(1)} %collective-permute-done.9.refs_1_, bf16[9,64,128]{2,1,0:T(8,128)(2,1)S(1)} %collective-permute-done.10.refs_2_, ...), custom_call_target="tpu_custom_call" | custom-call | bytes 4194304 | tf_op jit(solution)/shard_map/mean_out/pallas_call | solution.py:192
  83.0 12.8 %all-to-all-start.1 = ((bf16[16,64,1024]{2,1,0:T(8,128)(2,1)}), bf16[16,64,1024]{2,1,0:T(8,128)(2,1)S(1)}, u32[]{:S(2)}, u32[]{:S(2)}) async-start(bf16[16,64,1024]{2,1,0:T(8,128)(2,1)} %mean_out.1), calls=%async_computation.1 | async-start | bytes 4194304 | tf_op jit(solution)/shard_map/all_to_all | solution.py:411
  95.8 9.0 %gram.1 = bf16[8,2,128,1024]{3,2,1,0:T(8,128)(2,1)} custom-call(bf16[16,2,64,1024]{3,2,1,0:T(8,128)(2,1)} %all-to-all-done.grads), custom_call_target="tpu_custom_call" | custom-call | flops 8589934592 | bytes 8388608 | tf_op jit(solution)/shard_map/gram/pallas_call | solution.py:325
  104.9 19.8 %all-to-all-done.1 = bf16[16,64,1024]{2,1,0:T(8,128)(2,1)S(1)} async-done(((bf16[16,64,1024]{2,1,0:T(8,128)(2,1)}), bf16[16,64,1024]{2,1,0:T(8,128)(2,1)S(1)}, u32[]{:S(2)}, u32[]{:S(2)}) %all-to-all-start.1) | async-done | bytes 2097184 | tf_op jit(solution)/shard_map/all_to_all | solution.py:411
  124.7 8.9 %precond.1 = bf16[16,64,1024]{2,1,0:T(8,128)(2,1)} custom-call(s32[128]{0:T(128)} %get-tuple-element.17.table, bf16[1024,1024]{1,0:T(8,128)(2,1)S(1)} %bitcast.8, bf16[2,1024,1024]{2,1,0:T(8,128)(2,1)} %left.1, bf16[2,1024,1024]{2,1,0:T(8,128)(2,1)} %right.1), custom_call_target="tpu_custom_call" | custom-call | flops 85899345920 | bytes 8388608 | tf_op jit(solution)/shard_map/precond/pallas_call | solution.py:268
  133.6 29.6 %all_to_all.15.returned = bf16[16,64,1024]{2,1,0:T(8,128)(2,1)S(1)} all-to-all(bf16[16,64,1024]{2,1,0:T(8,128)(2,1)} %precond.1), channel_id=1, replica_groups=mesh['shard'=16,'z'=8,'core'=2] {'shard'}, dimensions={0} | all-to-all | bytes 4194304 | tf_op jit(solution)/shard_map/all_to_all | solution.py:418
  163.7 4.5 %collective-permute-done.15.swapped = bf16[16,64,1024]{2,1,0:T(8,128)(2,1)} collective-permute-done((bf16[16,64,1024]{2,1,0:T(8,128)(2,1)S(1)}, bf16[16,64,1024]{2,1,0:T(8,128)(2,1)}, u32[]{:S(2)}, u32[]{:S(2)}) %collective-permute-start.15) | collective-permute-done | bytes 2097184 | tf_op jit(solution)/shard_map/ppermute | solution.py:419
  168.2 1.0 copy-done.1
  169.3 4.3 %finish.1 = (bf16[18,64,1024]{2,1,0:T(8,128)(2,1)}, f32[2,2,64,1024]{3,2,1,0:T(8,128)}) custom-call(s32[128]{0:T(128)} %get-tuple-element.17.table, bf16[16,64,1024]{2,1,0:T(8,128)(2,1)S(1)} %all_to_all.15.returned, bf16[16,64,1024]{2,1,0:T(8,128)(2,1)} %collective-permute-done.15.swapped, bf16[2,128,1024]{2,1,0:T(8,128)(2,1)S(1)} %bitcast.10, ...), custom_call_target="tpu_custom_call" | custom-call | bytes 28311552 | tf_op jit(solution)/shard_map/finish/pallas_call | solution.py:370
  (23 shorter events, 4.1 us)
Async XLA Ops:
  7.2 3.1 %copy-start = (bf16[1,1152,1024]{2,1,0:T(8,128)(2,1)S(1)}, bf16[1,1152,1024]{2,1,0:T(8,128)(2,1)}, u32[]{:S(2)}) copy-start(bf16[1,1152,1024]{2,1,0:T(8,128)(2,1)} %param.5) | copy-start | bytes 7077892
  10.2 2.9 %collective-permute-start = (bf16[9,64,1024]{2,1,0:T(8,128)(2,1)S(1)}, bf16[9,64,1024]{2,1,0:T(8,128)(2,1)S(1)}, u32[]{:S(2)}, u32[]{:S(2)}) collective-permute-start(bf16[9,64,1024]{2,1,0:T(8,128)(2,1)S(1)} %get-tuple-element.18), channel_id=1, source_target_pairs={{0,1},{1,0},{2,3},{3,2},{4,5},{5,4},{6,7},{7,6},{8,9},{9,8},{10,11... | collective-permute-start | bytes 3538952 | tf_op jit(solution)/shard_map/ppermute | solution.py:401
  15.2 67.7 %all-to-all-start = ((bf16[16,2,64,1024]{3,2,1,0:T(8,128)(2,1)}), bf16[16,2,64,1024]{3,2,1,0:T(8,128)(2,1)}, u32[]{:S(2)}, u32[]{:S(2)}) async-start(bf16[16,2,64,1024]{3,2,1,0:T(8,128)(2,1)} %route_other.1), calls=%async_computation | async-start | bytes 8388608 | tf_op jit(solution)/shard_map/all_to_all | solution.py:405
  23.8 11.8 %collective-permute-start.1 = (bf16[9,64,128]{2,1,0:T(8,128)(2,1)S(1)}, bf16[9,64,128]{2,1,0:T(8,128)(2,1)S(1)}, u32[]{:S(2)}, u32[]{:S(2)}) collective-permute-start(bf16[9,64,128]{2,1,0:T(8,128)(2,1)S(1)} %get-tuple-element.20), channel_id=1, source_target_pairs={{0,8},{2,10},{4,12},{6,14},{8,0},{10,2},{12,4},{14,6},{1,9},{3,11}... | collective-permute-start | bytes 442376 | tf_op jit(solution)/shard_map/ppermute | solution.py:396
  28.3 18.3 %collective-permute-start.2 = (bf16[9,64,128]{2,1,0:T(8,128)(2,1)S(1)}, bf16[9,64,128]{2,1,0:T(8,128)(2,1)S(1)}, u32[]{:S(2)}, u32[]{:S(2)}) collective-permute-start(bf16[9,64,128]{2,1,0:T(8,128)(2,1)S(1)} %get-tuple-element.21), channel_id=1, source_target_pairs={{0,6},{2,8},{4,10},{6,12},{8,14},{10,0},{12,2},{14,4},{1,7},{3,9},... | collective-permute-start | bytes 442376 | tf_op jit(solution)/shard_map/ppermute | solution.py:396
  28.4 21.4 %collective-permute-start.3 = (bf16[9,64,128]{2,1,0:T(8,128)(2,1)S(1)}, bf16[9,64,128]{2,1,0:T(8,128)(2,1)S(1)}, u32[]{:S(2)}, u32[]{:S(2)}) collective-permute-start(bf16[9,64,128]{2,1,0:T(8,128)(2,1)S(1)} %get-tuple-element.22), channel_id=1, source_target_pairs={{0,10},{2,12},{4,14},{6,0},{8,2},{10,4},{12,6},{14,8},{1,11},{3,13... | collective-permute-start | bytes 442376 | tf_op jit(solution)/shard_map/ppermute | solution.py:396
  32.2 19.4 %collective-permute-start.4 = (bf16[9,64,128]{2,1,0:T(8,128)(2,1)S(1)}, bf16[9,64,128]{2,1,0:T(8,128)(2,1)S(1)}, u32[]{:S(2)}, u32[]{:S(2)}) collective-permute-start(bf16[9,64,128]{2,1,0:T(8,128)(2,1)S(1)} %get-tuple-element.23), channel_id=1, source_target_pairs={{0,4},{2,6},{4,8},{6,10},{8,12},{10,14},{12,0},{14,2},{1,5},{3,7},... | collective-permute-start | bytes 442376 | tf_op jit(solution)/shard_map/ppermute | solution.py:396
  32.9 18.7 %collective-permute-start.5 = (bf16[9,64,128]{2,1,0:T(8,128)(2,1)S(1)}, bf16[9,64,128]{2,1,0:T(8,128)(2,1)S(1)}, u32[]{:S(2)}, u32[]{:S(2)}) collective-permute-start(bf16[9,64,128]{2,1,0:T(8,128)(2,1)S(1)} %get-tuple-element.24), channel_id=1, source_target_pairs={{0,12},{2,14},{4,0},{6,2},{8,4},{10,6},{12,8},{14,10},{1,13},{3,15... | collective-permute-start | bytes 442376 | tf_op jit(solution)/shard_map/ppermute | solution.py:396
  35.6 19.5 %collective-permute-start.6 = (bf16[9,64,128]{2,1,0:T(8,128)(2,1)S(1)}, bf16[9,64,128]{2,1,0:T(8,128)(2,1)S(1)}, u32[]{:S(2)}, u32[]{:S(2)}) collective-permute-start(bf16[9,64,128]{2,1,0:T(8,128)(2,1)S(1)} %get-tuple-element.25), channel_id=1, source_target_pairs={{0,2},{2,4},{4,6},{6,8},{8,10},{10,12},{12,14},{14,0},{1,3},{3,5},... | collective-permute-start | bytes 442376 | tf_op jit(solution)/shard_map/ppermute | solution.py:396
  46.6 8.5 %collective-permute-start.7 = (bf16[9,64,128]{2,1,0:T(8,128)(2,1)S(1)}, bf16[9,64,128]{2,1,0:T(8,128)(2,1)S(1)}, u32[]{:S(2)}, u32[]{:S(2)}) collective-permute-start(bf16[9,64,128]{2,1,0:T(8,128)(2,1)S(1)} %get-tuple-element.26), channel_id=1, source_target_pairs={{0,14},{2,0},{4,2},{6,4},{8,6},{10,8},{12,10},{14,12},{1,15},{3,1}... | collective-permute-start | bytes 442376 | tf_op jit(solution)/shard_map/ppermute | solution.py:396
  55.3 10.7 %collective-permute-start.9 = (bf16[9,64,128]{2,1,0:T(8,128)(2,1)S(1)}, bf16[9,64,128]{2,1,0:T(8,128)(2,1)S(1)}, u32[]{:S(2)}, u32[]{:S(2)}) collective-permute-start(bf16[9,64,128]{2,1,0:T(8,128)(2,1)S(1)} %mean.1.refs_7_), channel_id=1, source_target_pairs={{0,12},{2,14},{4,0},{6,2},{8,4},{10,6},{12,8},{14,10},{1,13},{3,15... | collective-permute-start | bytes 442376 | tf_op jit(solution)/shard_map/ppermute | solution.py:396
  56.1 11.1 %collective-permute-start.8 = (bf16[9,64,128]{2,1,0:T(8,128)(2,1)S(1)}, bf16[9,64,128]{2,1,0:T(8,128)(2,1)S(1)}, u32[]{:S(2)}, u32[]{:S(2)}) collective-permute-start(bf16[9,64,128]{2,1,0:T(8,128)(2,1)S(1)} %mean.1.refs_7_), channel_id=1, source_target_pairs={{0,4},{2,6},{4,8},{6,10},{8,12},{10,14},{12,0},{14,2},{1,5},{3,7},... | collective-permute-start | bytes 442376 | tf_op jit(solution)/shard_map/ppermute | solution.py:396
  59.5 11.8 %collective-permute-start.11 = (bf16[9,64,128]{2,1,0:T(8,128)(2,1)S(1)}, bf16[9,64,128]{2,1,0:T(8,128)(2,1)S(1)}, u32[]{:S(2)}, u32[]{:S(2)}) collective-permute-start(bf16[9,64,128]{2,1,0:T(8,128)(2,1)S(1)} %mean.1.refs_7_), channel_id=1, source_target_pairs={{0,14},{2,0},{4,2},{6,4},{8,6},{10,8},{12,10},{14,12},{1,15},{3,1}... | collective-permute-start | bytes 442376 | tf_op jit(solution)/shard_map/ppermute | solution.py:396
  60.1 11.2 %collective-permute-start.10 = (bf16[9,64,128]{2,1,0:T(8,128)(2,1)S(1)}, bf16[9,64,128]{2,1,0:T(8,128)(2,1)S(1)}, u32[]{:S(2)}, u32[]{:S(2)}) collective-permute-start(bf16[9,64,128]{2,1,0:T(8,128)(2,1)S(1)} %mean.1.refs_7_), channel_id=1, source_target_pairs={{0,2},{2,4},{4,6},{6,8},{8,10},{10,12},{12,14},{14,0},{1,3},{3,5},... | collective-permute-start | bytes 442376 | tf_op jit(solution)/shard_map/ppermute | solution.py:396
  66.0 6.4 %collective-permute-start.14 = (bf16[9,64,128]{2,1,0:T(8,128)(2,1)S(1)}, bf16[9,64,128]{2,1,0:T(8,128)(2,1)S(1)}, u32[]{:S(2)}, u32[]{:S(2)}) collective-permute-start(bf16[9,64,128]{2,1,0:T(8,128)(2,1)S(1)} %collective-permute-done.9.refs_1_), channel_id=1, source_target_pairs={{0,14},{2,0},{4,2},{6,4},{8,6},{10,8},{12,10},{14,12},{1,15},{3,1}... | collective-permute-start | bytes 442376 | tf_op jit(solution)/shard_map/ppermute | solution.py:396
  67.2 7.4 %collective-permute-start.13 = (bf16[9,64,128]{2,1,0:T(8,128)(2,1)S(1)}, bf16[9,64,128]{2,1,0:T(8,128)(2,1)S(1)}, u32[]{:S(2)}, u32[]{:S(2)}) collective-permute-start(bf16[9,64,128]{2,1,0:T(8,128)(2,1)S(1)} %collective-permute-done.8.refs_0_), channel_id=1, source_target_pairs={{0,2},{2,4},{4,6},{6,8},{8,10},{10,12},{12,14},{14,0},{1,3},{3,5},... | collective-permute-start | bytes 442376 | tf_op jit(solution)/shard_map/ppermute | solution.py:396
  70.5 8.9 %collective-permute-start.12 = (bf16[9,64,128]{2,1,0:T(8,128)(2,1)S(1)}, bf16[9,64,128]{2,1,0:T(8,128)(2,1)S(1)}, u32[]{:S(2)}, u32[]{:S(2)}) collective-permute-start(bf16[9,64,128]{2,1,0:T(8,128)(2,1)S(1)} %collective-permute-done.8.refs_0_), channel_id=1, source_target_pairs={{0,4},{2,6},{4,8},{6,10},{8,12},{10,14},{12,0},{14,2},{1,5},{3,7},... | collective-permute-start | bytes 442376 | tf_op jit(solution)/shard_map/ppermute | solution.py:396
  83.0 41.7 %all-to-all-start.1 = ((bf16[16,64,1024]{2,1,0:T(8,128)(2,1)}), bf16[16,64,1024]{2,1,0:T(8,128)(2,1)S(1)}, u32[]{:S(2)}, u32[]{:S(2)}) async-start(bf16[16,64,1024]{2,1,0:T(8,128)(2,1)} %mean_out.1), calls=%async_computation.1 | async-start | bytes 4194304 | tf_op jit(solution)/shard_map/all_to_all | solution.py:411
  95.8 67.4 %reduce-scatter.2.cloned.1.call-start = ((), (), s32[]{:S(2)}) async-start(), calls=%async_computation.4 | async-start | bytes 4718592 | tf_op jit(solution)/shard_map/reduce_scatter | solution.py:415
  163.2 5.0 %collective-permute-start.15 = (bf16[16,64,1024]{2,1,0:T(8,128)(2,1)S(1)}, bf16[16,64,1024]{2,1,0:T(8,128)(2,1)}, u32[]{:S(2)}, u32[]{:S(2)}) collective-permute-start(bf16[16,64,1024]{2,1,0:T(8,128)(2,1)S(1)} %all_to_all.15.returned), channel_id=1, source_target_pairs={{0,1},{1,0},{2,3},{3,2},{4,5},{5,4},{6,7},{7,6},{8,9},{9,8},{10,11... | collective-permute-start | bytes 6291464 | tf_op jit(solution)/shard_map/ppermute | solution.py:419
  163.2 5.0 %collective-permute-start.16 = (bf16[2,128,1024]{2,1,0:T(8,128)(2,1)}, bf16[2,128,1024]{2,1,0:T(8,128)(2,1)S(1)}, u32[]{:S(2)}, u32[]{:S(2)}) collective-permute-start(bf16[2,128,1024]{2,1,0:T(8,128)(2,1)} %bitcast.9), channel_id=1, source_target_pairs={{0,1},{1,0},{2,3},{3,2},{4,5},{5,4},{6,7},{7,6},{8,9},{9,8},{10,11... | collective-permute-start | bytes 1572872 | tf_op jit(solution)/shard_map/ppermute | solution.py:419
  168.2 1.0 copy-start.1
Sparse Core Ops, SparseCore 0:
  105.0 56.7 reduce-scatter.1
